TPU v7x, 32 devices: a whole 2x2x4 slice. The times are simulated.
32 devices in a mesh: tile: 4 (over y, x), cand: 1, group: 8 (over z, core).
Axes of the slice: x: 2, y: 2, z: 4, core: 2. Of those that a mesh axis runs over, the one named last changes fastest.
Arguments:
- latent: bfloat16 [32, 12, 48, 384], P(('cand', 'group'), 'tile'), may hold values from -6 to 6
- gain_first: float32 [384], replicated, may hold values from 0.25 to 1.75
- weight_first: bfloat16 [3, 3, 1152, 384], P(None, None, 'group'), may hold values from -0.0625 to 0.0625
- bias_first: float32 [384], replicated, may hold values from -0.6 to 0.6
- gain_second: float32 [384], replicated, may hold values from 0.25 to 1.75
- weight_second: bfloat16 [3, 3, 1152, 384], P(None, None, 'group'), may hold values from -0.0625 to 0.0625
- bias_second: float32 [384], replicated, may hold values from -0.6 to 0.6
Outputs:
- decoded: bfloat16 [32, 12, 48, 384], P(('cand', 'group'), 'tile')
All inputs are finite; a program needn't handle non-finite values.
Results may differ from a plain program's by a relative error of at most 0.0042.
Values may be sent and summed in bfloat16 or wider, within the bound.
A program may use at most 128 MiB of HBM per device.

v0:
```python
import jax
import jax.numpy as jnp
from jax import lax
from jax.sharding import PartitionSpec as P


def shifted(value, axis, steps):
    count = lax.axis_size(axis)
    first, last = (max(0, -steps), min(count, count - steps))
    return lax.ppermute(value, axis, [(source, source + steps) for source in range(first, last)])


def with_halo(array, sides, width):
    for axis, dim in sides:
        size, length = (lax.axis_size(axis), array.shape[dim])
        up = [(i, (i + 1) % size) for i in range(size - 1)]
        down = [(j, i) for i, j in up]
        last = lax.slice_in_dim(array, length - width, length, axis=dim)
        first = lax.slice_in_dim(array, 0, width, axis=dim)
        before = lax.ppermute(last, axis, up)
        after = lax.ppermute(first, axis, down)
        array = jnp.concatenate([before, array, after], axis=dim)
    return array


def activate(values, gain):
    wide = values.astype(jnp.float32)
    scaled = wide * lax.rsqrt(jnp.mean(wide * wide, axis=-1, keepdims=True) + 1e-06) * gain
    return jax.nn.silu(scaled)


def widen(grown):
    across = grown.shape[2]
    padded = jnp.pad(grown, ((0, 0), (0, 0), (1, 1), (0, 0)))
    return jnp.concatenate([padded[:, :, k : k + across] for k in range(3)], axis=-1)


def taps(joined, piece):
    count = joined.shape[0] - 2
    tall = joined.shape[1] - 2
    across = joined.shape[2]
    inner = piece.shape[2]
    total = jnp.zeros((count * tall * across, piece.shape[3]), jnp.float32)
    for step_t in range(3):
        for step_r in range(3):
            window = joined[step_t : step_t + count, step_r : step_r + tall].reshape(-1, inner)
            total = total + jnp.dot(
                window, piece[step_t, step_r], preferred_element_type=jnp.float32
            )
    return total.reshape(count, tall, across, piece.shape[3])


def local(latent, gain_first, weight_first, bias_first, gain_second, weight_second, bias_second):
    frames, rows, width, chans = latent.shape
    depth = 1
    first = activate(latent, gain_first).astype(jnp.bfloat16)
    earlier = shifted(first[frames - 2 :], "group", 1)
    stacked = jnp.concatenate([earlier, first], axis=0)
    grown = with_halo(stacked, (("tile", 1),), depth)
    joined_first = widen(grown)
    hidden = (
        taps(joined_first, lax.all_gather(weight_first, "group", axis=2, tiled=True)) + bias_first
    )
    second = activate(hidden, gain_second)
    second = second.astype(jnp.bfloat16)
    later = shifted(second[frames - 2 :], "group", 1)
    second = jnp.concatenate([later, second], axis=0)
    second = with_halo(second, (("tile", 1),), 1)
    joined_second = widen(second)
    branch = taps(joined_second, lax.all_gather(weight_second, "group", axis=2, tiled=True))
    result = latent.astype(jnp.float32) + branch + bias_second
    return result.astype(jnp.bfloat16)


def solution(mesh):
    return jax.shard_map(
        local,
        mesh=mesh,
        in_specs=(
            P(("cand", "group"), "tile", None, None),
            P(),
            P(None, None, "group", None),
            P(),
            P(),
            P(None, None, "group", None),
            P(),
        ),
        out_specs=P(("cand", "group"), "tile", None, None),
        check_vma=False,
    )
```

profile of v0, /device:TPU:27, one launch (start us, length us, event | category | flops | bytes accessed | tf_op | source)
XLA Modules:
  0.0 188.7 jit_solution(3821670526623363480)
XLA Ops:
  6.5 0.7 all-gather.3.cloned.1.call-update
  7.3 0.7 all-gather.5.cloned.1.call-update
  8.6 1.3 collective-permute-start
  9.9 2.2 %collective-permute-done = bf16[2,3,48,384]{3,2,1,0:T(8,128)(2,1)S(1)} collective-permute-done((bf16[2,3,48,384]{3,2,1,0:T(8,128)(2,1)S(1)}, bf16[2,3,48,384]{3,2,1,0:T(8,128)(2,1)S(1)}, u32[]{:S(2)}, u32[]{:S(2)}) %collective-permute-start) | collective-permute-done | bytes 221216 | tf_op jit(solution)/shard_map/ppermute | solution.py:10
  12.2 3.1 %collective-permute-start.1 = (bf16[6,1,48,384]{3,2,1,0:T(8,128)(2,1)S(1)}, bf16[6,1,48,384]{3,2,1,0:T(8,128)(2,1)S(1)}, u32[]{:S(2)}, u32[]{:S(2)}) collective-permute-start(bf16[6,1,48,384]{3,2,1,0:T(8,128)(2,1)S(1)} %get-tuple-element.29), channel_id=1, source_target_pairs={{0,8},{8,16},{16,24},{1,9},{9,17},{17,25},{2,10},{10,18},{18,26},{... | collective-permute-start | bytes 663560 | tf_op jit(solution)/shard_map/ppermute | solution.py:20
  15.3 2.2 %collective-permute-start.2 = (bf16[6,1,48,384]{3,2,1,0:T(8,128)(2,1)S(1)}, bf16[6,1,48,384]{3,2,1,0:T(8,128)(2,1)S(1)}, u32[]{:S(2)}, u32[]{:S(2)}) collective-permute-start(bf16[6,1,48,384]{3,2,1,0:T(8,128)(2,1)S(1)} %get-tuple-element.30), channel_id=1, source_target_pairs={{8,0},{16,8},{24,16},{9,1},{17,9},{25,17},{10,2},{18,10},{26,18},{... | collective-permute-start | bytes 663560 | tf_op jit(solution)/shard_map/ppermute | solution.py:21
  17.5 1.4 collective-permute-done.1
  18.9 5.0 %collective-permute-done.2 = bf16[6,1,48,384]{3,2,1,0:T(8,128)(2,1)S(1)} collective-permute-done((bf16[6,1,48,384]{3,2,1,0:T(8,128)(2,1)S(1)}, bf16[6,1,48,384]{3,2,1,0:T(8,128)(2,1)S(1)}, u32[]{:S(2)}, u32[]{:S(2)}) %collective-permute-start.2) | collective-permute-done | bytes 221216 | tf_op jit(solution)/shard_map/ppermute | solution.py:21
  23.8 0.6 fusion.16
  24.4 0.6 fusion.54
  25.5 3.6 %fusion.52 = (bf16[4,3,48,1152]{3,2,1,0:T(8,128)(2,1)S(1)}, bf16[4,3,48,1152]{3,2,1,0:T(8,128)(2,1)}, bf16[4,3,48,1152]{3,2,1,0:T(8,128)(2,1)}, bf16[4,3,48,1152...) fusion(bf16[6,5,48,1152]{3,2,1,0:T(8,128)(2,1)S(1)} %pad_maximu, ...), kind=kLoop, calls=%fused_computation.89 | loop fusion | bytes 23887872 | tf_op jit(solution)/shard_map/slice | solution.py:46
  29.1 57.4 %all-gather.3.cloned.1.call-done = bf16[3,3,1152,384]{3,2,1,0:T(8,128)(2,1)} async-done(((bf16[3,3,144,384]{3,2,1,0:T(8,128)(2,1)}), bf16[3,3,1152,384]{3,2,1,0:T(8,128)(2,1)}) %all-gather.3.cloned.1.call-update) | async-done | bytes 7962640 | tf_op jit(solution)/shard_map/all_gather | solution.py:62
  86.4 2.6 %fusion.43 = f32[576,384]{1,0:T(8,128)S(1)} fusion(bf16[576,1152]{1,0:T(8,128)(2,1)} %bitcast.112, bf16[3,3,1152,384]{3,2,1,0:T(8,128)(2,1)} %all-gather.3.cloned.1.call-done), kind=kOutput, calls=%fused_computation.64 | convolution fusion | flops 509607936 | bytes 3096576 | tf_op jit(solution)/shard_map/dot_general | solution.py:47
  89.1 2.8 %fusion.44 = f32[576,384]{1,0:T(8,128)S(1)} fusion(bf16[576,1152]{1,0:T(8,128)(2,1)S(1)} %bitcast.110, bf16[3,3,1152,384]{3,2,1,0:T(8,128)(2,1)} %all-gather.3.cloned.1.call-done), kind=kOutput, calls=%fused_computation.66 | convolution fusion | flops 509607936 | bytes 3096576 | tf_op jit(solution)/shard_map/dot_general | solution.py:47
  91.9 0.9 fusion.45
  93.2 0.9 fusion.46
  94.1 0.4 copy-done.5
  94.5 0.9 fusion.47
  95.4 0.5 copy-done.3
  95.8 0.9 fusion.48
  96.7 0.6 copy-done.1
  97.3 0.9 fusion.49
  98.2 0.9 fusion.50
  99.1 1.3 multiply_reduce_fusion
  100.9 1.3 collective-permute-start.3
  102.2 2.1 %collective-permute-done.3 = bf16[2,3,48,384]{3,2,1,0:T(8,128)(2,1)S(1)} collective-permute-done((bf16[2,3,48,384]{3,2,1,0:T(8,128)(2,1)S(1)}, bf16[2,3,48,384]{3,2,1,0:T(8,128)(2,1)S(1)}, u32[]{:S(2)}, u32[]{:S(2)}) %collective-permute-start.3) | collective-permute-done | bytes 221216 | tf_op jit(solution)/shard_map/ppermute | solution.py:10
  104.3 3.1 %collective-permute-start.4 = (bf16[6,1,48,384]{3,2,1,0:T(8,128)(2,1)S(1)}, bf16[6,1,48,384]{3,2,1,0:T(8,128)(2,1)S(1)}, u32[]{:S(2)}, u32[]{:S(2)}) collective-permute-start(bf16[6,1,48,384]{3,2,1,0:T(8,128)(2,1)S(1)} %get-tuple-element.27), channel_id=1, source_target_pairs={{0,8},{8,16},{16,24},{1,9},{9,17},{17,25},{2,10},{10,18},{18,26},{... | collective-permute-start | bytes 663560 | tf_op jit(solution)/shard_map/ppermute | solution.py:20
  107.4 2.4 %collective-permute-start.5 = (bf16[6,1,48,384]{3,2,1,0:T(8,128)(2,1)S(1)}, bf16[6,1,48,384]{3,2,1,0:T(8,128)(2,1)S(1)}, u32[]{:S(2)}, u32[]{:S(2)}) collective-permute-start(bf16[6,1,48,384]{3,2,1,0:T(8,128)(2,1)S(1)} %get-tuple-element.28), channel_id=1, source_target_pairs={{8,0},{16,8},{24,16},{9,1},{17,9},{25,17},{10,2},{18,10},{26,18},{... | collective-permute-start | bytes 663560 | tf_op jit(solution)/shard_map/ppermute | solution.py:21
  109.8 1.6 collective-permute-done.4
  111.4 4.0 %collective-permute-done.5 = bf16[6,1,48,384]{3,2,1,0:T(8,128)(2,1)S(1)} collective-permute-done((bf16[6,1,48,384]{3,2,1,0:T(8,128)(2,1)S(1)}, bf16[6,1,48,384]{3,2,1,0:T(8,128)(2,1)S(1)}, u32[]{:S(2)}, u32[]{:S(2)}) %collective-permute-start.5) | collective-permute-done | bytes 221216 | tf_op jit(solution)/shard_map/ppermute | solution.py:21
  115.4 0.6 select_maximum_fusion
  116.0 0.6 fusion.53
  117.0 3.6 %fusion.51 = (bf16[4,3,48,1152]{3,2,1,0:T(8,128)(2,1)S(1)}, bf16[4,3,48,1152]{3,2,1,0:T(8,128)(2,1)}, bf16[4,3,48,1152]{3,2,1,0:T(8,128)(2,1)}, bf16[4,3,48,1152...) fusion(bf16[6,5,48,1152]{3,2,1,0:T(8,128)(2,1)S(1)} %pad_maximu, ...), kind=kLoop, calls=%fused_computation.88 | loop fusion | bytes 23887872 | tf_op jit(solution)/shard_map/slice | solution.py:46
  120.6 46.8 %all-gather.5.cloned.1.call-done = bf16[3,3,1152,384]{3,2,1,0:T(8,128)(2,1)} async-done(((bf16[3,3,144,384]{3,2,1,0:T(8,128)(2,1)}), bf16[3,3,1152,384]{3,2,1,0:T(8,128)(2,1)}) %all-gather.5.cloned.1.call-update) | async-done | bytes 7962640 | tf_op jit(solution)/shard_map/all_gather | solution.py:70
  167.4 2.6 %fusion.35 = f32[576,384]{1,0:T(8,128)S(1)} fusion(bf16[576,1152]{1,0:T(8,128)(2,1)} %bitcast.113, bf16[3,3,1152,384]{3,2,1,0:T(8,128)(2,1)} %all-gather.5.cloned.1.call-done), kind=kOutput, calls=%fused_computation.47 | convolution fusion | flops 509607936 | bytes 3096576 | tf_op jit(solution)/shard_map/dot_general | solution.py:47
  170.0 2.8 %fusion.36 = f32[576,384]{1,0:T(8,128)S(1)} fusion(bf16[576,1152]{1,0:T(8,128)(2,1)S(1)} %bitcast.111, bf16[3,3,1152,384]{3,2,1,0:T(8,128)(2,1)} %all-gather.5.cloned.1.call-done), kind=kOutput, calls=%fused_computation.49 | convolution fusion | flops 509607936 | bytes 3096576 | tf_op jit(solution)/shard_map/dot_general | solution.py:47
  172.8 0.9 fusion.37
  173.7 0.4 copy-done.8
  174.2 0.9 fusion.38
  175.0 0.4 copy-done.6
  175.5 0.9 fusion.39
  176.4 0.4 copy-done.4
  176.8 0.9 fusion.40
  177.7 0.4 copy-done.2
  178.1 0.9 fusion.41
  179.0 0.9 fusion.42
  179.9 1.1 fusion.21
  181.0 0.9 fusion.34
  (45 shorter events, 2.3 us)
Async XLA Ops:
  6.5 1.5 copy-start
  6.5 1.7 copy-start.16
  6.5 79.9 %all-gather.3.cloned.1.call-start = ((), (), s32[]{:S(2)}) async-start(), calls=%async_computation | async-start | bytes 8957952 | tf_op jit(solution)/shard_map/all_gather | solution.py:62
  7.3 160.2 %all-gather.5.cloned.1.call-start = ((), (), s32[]{:S(2)}) async-start(), calls=%async_computation.1 | async-start | bytes 8957952 | tf_op jit(solution)/shard_map/all_gather | solution.py:70
  8.6 3.5 %collective-permute-start = (bf16[2,3,48,384]{3,2,1,0:T(8,128)(2,1)S(1)}, bf16[2,3,48,384]{3,2,1,0:T(8,128)(2,1)S(1)}, u32[]{:S(2)}, u32[]{:S(2)}) collective-permute-start(bf16[2,3,48,384]{3,2,1,0:T(8,128)(2,1)S(1)} %slice.186), channel_id=1, source_target_pairs={{0,1},{1,2},{2,3},{3,4},{4,5},{5,6},{6,7},{8,9},{9,10},{10,11},{11... | collective-permute-start | bytes 663560 | tf_op jit(solution)/shard_map/ppermute | solution.py:10
  12.2 6.7 %collective-permute-start.1 = (bf16[6,1,48,384]{3,2,1,0:T(8,128)(2,1)S(1)}, bf16[6,1,48,384]{3,2,1,0:T(8,128)(2,1)S(1)}, u32[]{:S(2)}, u32[]{:S(2)}) collective-permute-start(bf16[6,1,48,384]{3,2,1,0:T(8,128)(2,1)S(1)} %get-tuple-element.29), channel_id=1, source_target_pairs={{0,8},{8,16},{16,24},{1,9},{9,17},{17,25},{2,10},{10,18},{18,26},{... | collective-permute-start | bytes 663560 | tf_op jit(solution)/shard_map/ppermute | solution.py:20
  15.3 8.5 %collective-permute-start.2 = (bf16[6,1,48,384]{3,2,1,0:T(8,128)(2,1)S(1)}, bf16[6,1,48,384]{3,2,1,0:T(8,128)(2,1)S(1)}, u32[]{:S(2)}, u32[]{:S(2)}) collective-permute-start(bf16[6,1,48,384]{3,2,1,0:T(8,128)(2,1)S(1)} %get-tuple-element.30), channel_id=1, source_target_pairs={{8,0},{16,8},{24,16},{9,1},{17,9},{25,17},{10,2},{18,10},{26,18},{... | collective-permute-start | bytes 663560 | tf_op jit(solution)/shard_map/ppermute | solution.py:21
  86.4 2.6 %copy-start.11 = (bf16[4,3,48,1152]{3,2,1,0:T(8,128)(2,1)S(1)}, bf16[4,3,48,1152]{3,2,1,0:T(8,128)(2,1)}, u32[]{:S(2)}) copy-start(bf16[4,3,48,1152]{3,2,1,0:T(8,128)(2,1)} %get-tuple-element.16) | copy-start | bytes 3981316
  86.4 5.4 %copy-start.14 = (bf16[3,3,1152,384]{3,2,1,0:T(8,128)(2,1)S(1)}, bf16[3,3,1152,384]{3,2,1,0:T(8,128)(2,1)}, u32[]{:S(2)}) copy-start(bf16[3,3,1152,384]{3,2,1,0:T(8,128)(2,1)} %all-gather.3.cloned.1.call-done) | copy-start | bytes 23887876
  89.1 2.8 %copy-start.9 = (bf16[4,3,48,1152]{3,2,1,0:T(8,128)(2,1)S(1)}, bf16[4,3,48,1152]{3,2,1,0:T(8,128)(2,1)}, u32[]{:S(2)}) copy-start(bf16[4,3,48,1152]{3,2,1,0:T(8,128)(2,1)} %get-tuple-element.17) | copy-start | bytes 3981316
  91.9 1.3 copy-start.7
  93.2 1.3 copy-start.5
  94.5 1.3 copy-start.3
  95.8 1.4 copy-start.1
  98.2 0.9 copy-start.15
  99.1 1.4 copy-start.17
  100.9 3.4 %collective-permute-start.3 = (bf16[2,3,48,384]{3,2,1,0:T(8,128)(2,1)S(1)}, bf16[2,3,48,384]{3,2,1,0:T(8,128)(2,1)S(1)}, u32[]{:S(2)}, u32[]{:S(2)}) collective-permute-start(bf16[2,3,48,384]{3,2,1,0:T(8,128)(2,1)S(1)} %slice.207), channel_id=1, source_target_pairs={{0,1},{1,2},{2,3},{3,4},{4,5},{5,6},{6,7},{8,9},{9,10},{10,11},{11... | collective-permute-start | bytes 663560 | tf_op jit(solution)/shard_map/ppermute | solution.py:10
  104.3 7.1 %collective-permute-start.4 = (bf16[6,1,48,384]{3,2,1,0:T(8,128)(2,1)S(1)}, bf16[6,1,48,384]{3,2,1,0:T(8,128)(2,1)S(1)}, u32[]{:S(2)}, u32[]{:S(2)}) collective-permute-start(bf16[6,1,48,384]{3,2,1,0:T(8,128)(2,1)S(1)} %get-tuple-element.27), channel_id=1, source_target_pairs={{0,8},{8,16},{16,24},{1,9},{9,17},{17,25},{2,10},{10,18},{18,26},{... | collective-permute-start | bytes 663560 | tf_op jit(solution)/shard_map/ppermute | solution.py:20
  107.4 8.0 %collective-permute-start.5 = (bf16[6,1,48,384]{3,2,1,0:T(8,128)(2,1)S(1)}, bf16[6,1,48,384]{3,2,1,0:T(8,128)(2,1)S(1)}, u32[]{:S(2)}, u32[]{:S(2)}) collective-permute-start(bf16[6,1,48,384]{3,2,1,0:T(8,128)(2,1)S(1)} %get-tuple-element.28), channel_id=1, source_target_pairs={{8,0},{16,8},{24,16},{9,1},{17,9},{25,17},{10,2},{18,10},{26,18},{... | collective-permute-start | bytes 663560 | tf_op jit(solution)/shard_map/ppermute | solution.py:21
  167.4 2.6 %copy-start.12 = (bf16[4,3,48,1152]{3,2,1,0:T(8,128)(2,1)S(1)}, bf16[4,3,48,1152]{3,2,1,0:T(8,128)(2,1)}, u32[]{:S(2)}) copy-start(bf16[4,3,48,1152]{3,2,1,0:T(8,128)(2,1)} %get-tuple-element.7) | copy-start | bytes 3981316
  167.4 5.4 %copy-start.13 = (bf16[3,3,1152,384]{3,2,1,0:T(8,128)(2,1)S(1)}, bf16[3,3,1152,384]{3,2,1,0:T(8,128)(2,1)}, u32[]{:S(2)}) copy-start(bf16[3,3,1152,384]{3,2,1,0:T(8,128)(2,1)} %all-gather.5.cloned.1.call-done) | copy-start | bytes 23887876
  170.0 2.8 %copy-start.10 = (bf16[4,3,48,1152]{3,2,1,0:T(8,128)(2,1)S(1)}, bf16[4,3,48,1152]{3,2,1,0:T(8,128)(2,1)}, u32[]{:S(2)}) copy-start(bf16[4,3,48,1152]{3,2,1,0:T(8,128)(2,1)} %get-tuple-element.8) | copy-start | bytes 3981316
  172.8 1.3 copy-start.8
  174.2 1.3 copy-start.6
  175.5 1.3 copy-start.4
  176.8 1.3 copy-start.2
  179.9 1.1 copy-start.18
Sparse Core Ops, SparseCore 0:
  9.0 77.4 all-gather.2
  88.0 79.3 all-gather.4
where the time goes:
time: 191 us; the launch traced here: 189 us
  waiting for transfers between devices  122 us (64%)
  matrix products  23.5 us (12%)
  between operations  13.8 us (7%)
  starting transfers between devices  13.4 us (7%)
  local copies, waits for them, and re-layouts  12.4 us (6%)
  other arithmetic  3.79 us (2%)
    all_gather x1, waiting for transfers between devices, local(): lax.all_gather(weight_first, 'group', axis=2, tiled=True)  57.4 us
    all_gather x1, waiting for transfers between devices, local(): lax.all_gather(weight_second, 'group', axis=2, tiled=True)  46.8 us
    dot_general x18, matrix products, taps(): jnp.dot(window, piece[step_t, step_r], preferred_element_type=jnp.float32)  23.5 us
    ppermute x2, waiting for transfers between devices, with_halo(): after = lax.ppermute(first, axis, down)  8.96 us
    slice x2, local copies, waits for them, and re-layouts, taps(): joined[step_t:step_t + count, step_r:step_r + tall].reshape(-1, inner)  7.24 us
    ppermute x2, starting transfers between devices, with_halo(): before = lax.ppermute(last, axis, up)  6.22 us
    ppermute x2, starting transfers between devices, with_halo(): after = lax.ppermute(first, axis, down)  4.55 us
    ppermute x2, waiting for transfers between devices, shifted(): lax.ppermute(value, axis, [(source, source + steps) for source in range(f...  4.32 us
  transfers between devices with their start and end apart: 8, of which 8 were waited for; matrix products, arithmetic and copies ran while one was open for 12% of the time, Pallas kernels for 0%

commit v1 on v0

--- a/solution.py
+++ b/solution.py
@@ -1,6 +1,8 @@
 import jax
 import jax.numpy as jnp
 from jax import lax
+from jax.experimental import pallas as pl
+from jax.experimental.pallas import tpu as pltpu
 from jax.sharding import PartitionSpec as P
 
 
@@ -72,9 +74,380 @@
     return result.astype(jnp.bfloat16)
 
 
+BF16, F32 = jnp.bfloat16, jnp.float32
+MESH = pl.DeviceIdType.MESH
+UNITS = 6
+
+
+def act_slab(wide, gain):
+    square = jnp.sum(wide * wide, axis=-1, keepdims=True) * (1.0 / wide.shape[-1])
+    scaled = wide * lax.rsqrt(square + 1e-06) * gain
+    return scaled / (1.0 + jnp.exp(-scaled))
+
+
+def fused(
+    latent, gain_first, weight_first, bias_first, gain_second, weight_second, bias_second, out,
+    taps_all, lat, sec, cols, total,
+    load_sem, lat_sem, z_send, z_recv, xy_send, xy_recv, core_send, core_recv, halo_send, halo_recv,
+):
+    tile, group = lax.axis_index("tile"), lax.axis_index("group")
+    tiles, groups = lax.axis_size("tile"), lax.axis_size("group")
+    y, x = tile // 2, tile % 2
+    z, core = group // 2, group % 2
+    zs = groups // 2
+    frames, rows, across, chans = latent.shape
+    x_tile, y_tile = 2 * y + (1 - x), 2 * (1 - y) + x
+    z_part = x + 2 * y - 3 * x * y
+    x_part = x + 2 * y - 2 * x * y
+    y_part = x + 2 * y - x * y
+    corner = (x + y) == 2
+
+    lat[...] = jnp.zeros_like(lat)
+    sec[...] = jnp.zeros_like(sec)
+    total[...] = jnp.zeros_like(total)
+
+    def load(unit):
+        source = weight_first if unit < 3 else weight_second
+        return pltpu.make_async_copy(
+            source.at[pl.ds(3 * (unit % 3), 3)],
+            taps_all.at[pl.ds(3 * unit, 3), z, core],
+            load_sem.at[unit],
+        )
+
+    lat_copy = pltpu.make_async_copy(
+        latent, lat.at[pl.ds(2, frames), pl.ds(1, rows)], lat_sem
+    )
+    for unit in range(UNITS):
+        load(unit).start()
+    lat_copy.start()
+
+    barrier = pltpu.get_barrier_semaphore()
+    partners = [
+        ({"group": group + 2}, z < zs - 1),
+        ({"group": group - 2}, z > 0),
+        ({"group": group + 1}, group < groups - 1),
+        ({"group": group - 1}, group > 0),
+        ({"tile": tile + 1}, tile < tiles - 1),
+        ({"tile": tile - 1}, tile > 0),
+        ({"tile": x_tile}, None),
+        ({"tile": y_tile}, None),
+    ]
+    expected = 0
+    for where, there in partners:
+        if there is None:
+            pl.semaphore_signal(barrier, inc=1, device_id=where, device_id_type=MESH)
+            expected = expected + 1
+        else:
+            @pl.when(there)
+            def _():
+                pl.semaphore_signal(barrier, inc=1, device_id=where, device_id_type=MESH)
+            expected = expected + there.astype(jnp.int32)
+    pl.semaphore_wait(barrier, expected)
+
+    def piece(unit, part, origin, where, send, recv):
+        block = taps_all.at[3 * unit + part, origin, core]
+        return pltpu.make_async_remote_copy(
+            src_ref=block, dst_ref=block, send_sem=send, recv_sem=recv,
+            device_id=where, device_id_type=MESH,
+        )
+
+    def up(unit, dist):
+        return piece(unit, z_part, z - dist, {"group": group + 2}, z_send.at[unit, 0, dist], z_recv.at[unit, 0, dist])
+
+    def down(unit, dist):
+        return piece(unit, z_part, z + dist, {"group": group - 2}, z_send.at[unit, 1, dist], z_recv.at[unit, 1, dist])
+
+    def along_x(unit, step):
+        return piece(unit, x_part, (z + step) % zs, {"tile": x_tile}, xy_send.at[unit, 0, step - 1], xy_recv.at[unit, 0, step - 1])
+
+    def along_y(unit, step):
+        return piece(unit, y_part, (z + step) % zs, {"tile": y_tile}, xy_send.at[unit, 1, step - 1], xy_recv.at[unit, 1, step - 1])
+
+    def across_cores(unit):
+        block = taps_all.at[pl.ds(3 * unit, 3), :, core]
+        return pltpu.make_async_remote_copy(
+            src_ref=block, dst_ref=block, send_sem=core_send.at[unit], recv_sem=core_recv.at[unit],
+            device_id={"group": 2 * z + (1 - core)}, device_id_type=MESH,
+        )
+
+    def own(unit):
+        @pl.when(z < zs - 1)
+        def _():
+            up(unit, 0).start()
+
+        @pl.when(z > 0)
+        def _():
+            down(unit, 0).start()
+
+    def hand_on(unit, step):
+        @pl.when(jnp.logical_not(corner))
+        def _():
+            along_x(unit, step).start()
+            along_y(unit, step).start()
+
+    def arrived(unit, dist):
+        @pl.when(z >= dist)
+        def _():
+            up(unit, dist - 1).wait_recv()
+            if dist < zs - 1:
+                @pl.when(z < zs - 1)
+                def _():
+                    up(unit, dist).start()
+            hand_on(unit, zs - dist)
+
+        @pl.when(z + dist < zs)
+        def _():
+            down(unit, dist - 1).wait_recv()
+            if dist < zs - 1:
+                @pl.when(z > 0)
+                def _():
+                    down(unit, dist).start()
+            hand_on(unit, dist)
+
+    def frame_copy(buf, which):
+        return pltpu.make_async_remote_copy(
+            src_ref=buf.at[pl.ds(frames, 2), pl.ds(1, rows)], dst_ref=buf.at[pl.ds(0, 2), pl.ds(1, rows)],
+            send_sem=halo_send.at[which, 0], recv_sem=halo_recv.at[which, 0],
+            device_id={"group": group + 1}, device_id_type=MESH,
+        )
+
+    def row_copy(buf, which, later):
+        return pltpu.make_async_remote_copy(
+            src_ref=buf.at[:, rows if later else 1], dst_ref=buf.at[:, 0 if later else rows + 1],
+            send_sem=halo_send.at[which, 1 + later], recv_sem=halo_recv.at[which, 1 + later],
+            device_id={"tile": tile + 1 if later else tile - 1}, device_id_type=MESH,
+        )
+
+    def send_frames(buf, which):
+        @pl.when(group < groups - 1)
+        def _():
+            frame_copy(buf, which).start()
+
+    def send_rows(buf, which):
+        @pl.when(group > 0)
+        def _():
+            frame_copy(buf, which).wait_recv()
+
+        @pl.when(tile < tiles - 1)
+        def _():
+            row_copy(buf, which, 1).start()
+
+        @pl.when(tile > 0)
+        def _():
+            row_copy(buf, which, 0).start()
+
+    def await_rows(buf, which):
+        @pl.when(tile > 0)
+        def _():
+            row_copy(buf, which, 1).wait_recv()
+
+        @pl.when(tile < tiles - 1)
+        def _():
+            row_copy(buf, which, 0).wait_recv()
+
+    column = lax.broadcasted_iota(jnp.int32, (across, chans), 0)
+
+    def spread(frame, row, value):
+        before = jnp.where(column == 0, 0.0, pltpu.roll(value, 1, 0))
+        after = jnp.where(column == across - 1, 0.0, pltpu.roll(value, across - 1, 0))
+        cols[frame, row, :, 0:chans] = before.astype(BF16)
+        cols[frame, row, :, chans : 2 * chans] = value.astype(BF16)
+        cols[frame, row, :, 2 * chans : 3 * chans] = after.astype(BF16)
+
+    def first_columns():
+        def step(frame, carry):
+            for row in range(rows + 2):
+                spread(frame, row, act_slab(lat[frame, row].astype(F32), gain_first[...]))
+            return carry
+        lax.fori_loop(0, frames + 2, step, 0)
+
+    def second_values():
+        def step(frame, carry):
+            for row in range(rows):
+                hidden = total[frame, row] + bias_first[...]
+                sec[frame + 2, row + 1] = act_slab(hidden, gain_second[...]).astype(BF16)
+            return carry
+        lax.fori_loop(0, frames, step, 0)
+        total[...] = jnp.zeros_like(total)
+
+    def second_columns():
+        def step(frame, carry):
+            for row in range(rows + 2):
+                spread(frame, row, sec[frame, row].astype(F32))
+            return carry
+        lax.fori_loop(0, frames + 2, step, 0)
+
+    def multiply(unit):
+        step_t = unit % 3
+
+        def step(step_r, carry):
+            window = cols[pl.ds(step_t, frames), pl.ds(step_r, rows)].reshape(-1, 3 * chans)
+            weight = taps_all[3 * unit + step_r].reshape(3 * chans, chans)
+            added = jnp.dot(window, weight, preferred_element_type=F32)
+            total[...] += added.reshape(frames, rows, across, chans)
+            return carry
+        lax.fori_loop(0, 3, step, 0)
+
+    load(0).wait()
+    own(0)
+    lat_copy.wait()
+    send_frames(lat, 0)
+    for unit in range(1, UNITS):
+        load(unit).wait()
+
+    def stage(index, lag, body):
+        unit = index - lag
+
+        @pl.when((unit >= 0) & (unit < UNITS))
+        def _():
+            body(unit)
+
+    def direct(unit):
+        for step in range(1, zs):
+            @pl.when(tile != 2)
+            def _():
+                along_x(unit, step).wait_recv()
+
+            @pl.when(tile != 1)
+            def _():
+                along_y(unit, step).wait_recv()
+
+            @pl.when(corner)
+            def _():
+                along_x(unit, step).start()
+                along_y(unit, step).start()
+
+    def forwarded(unit):
+        for step in range(1, zs):
+            @pl.when(tile == 2)
+            def _():
+                along_x(unit, step).wait_recv()
+
+            @pl.when(tile == 1)
+            def _():
+                along_y(unit, step).wait_recv()
+        across_cores(unit).start()
+
+    def compute(unit):
+        across_cores(unit).wait_recv()
+        multiply(unit)
+
+    lag = zs + 1
+    def turn(index, carry):
+        stage(index, -1, own)
+        for dist in range(1, zs):
+            stage(index, dist - 1, lambda unit: arrived(unit, dist))
+
+        @pl.when(index == 0)
+        def _():
+            send_rows(lat, 0)
+
+        @pl.when(index == 2)
+        def _():
+            await_rows(lat, 0)
+            first_columns()
+
+        @pl.when(index == lag + 3)
+        def _():
+            send_rows(sec, 1)
+
+        stage(index, zs - 1, direct)
+        stage(index, zs, forwarded)
+
+        @pl.when(index == lag + 3)
+        def _():
+            await_rows(sec, 1)
+            second_columns()
+
+        stage(index, lag, compute)
+
+        @pl.when(index == lag + 2)
+        def _():
+            second_values()
+            send_frames(sec, 1)
+        return carry
+
+    lax.fori_loop(0, UNITS + lag, turn, 0)
+
+    def finish(frame, carry):
+        for row in range(rows):
+            value = lat[frame + 2, row + 1].astype(F32) + total[frame, row] + bias_second[...]
+            out[frame, row] = value.astype(BF16)
+        return carry
+    lax.fori_loop(0, frames, finish, 0)
+
+    def drain(unit, carry):
+        for dist in range(zs - 1):
+            @pl.when((z >= dist) & (z < zs - 1))
+            def _():
+                up(unit, dist).wait_send()
+
+            @pl.when((z + dist < zs) & (z > 0))
+            def _():
+                down(unit, dist).wait_send()
+        for step in range(1, zs):
+            along_x(unit, step).wait_send()
+            along_y(unit, step).wait_send()
+        across_cores(unit).wait_send()
+        return carry
+    lax.fori_loop(0, UNITS, drain, 0)
+    for which, buf in enumerate((lat, sec)):
+        @pl.when(group < groups - 1)
+        def _():
+            frame_copy(buf, which).wait_send()
+
+        @pl.when(tile < tiles - 1)
+        def _():
+            row_copy(buf, which, 1).wait_send()
+
+        @pl.when(tile > 0)
+        def _():
+            row_copy(buf, which, 0).wait_send()
+
+
+def fused_local(latent, gain_first, weight_first, bias_first, gain_second, weight_second, bias_second):
+    frames, rows, across, chans = latent.shape
+    depth, zs = weight_first.shape[2], lax.axis_size("group") // 2
+    line = lambda values: values.reshape(1, chans)
+    flat = lambda weight: weight.reshape(9, depth, chans)
+    vmem, anywhere = pl.BlockSpec(memory_space=pltpu.VMEM), pl.BlockSpec(memory_space=pl.ANY)
+    return pl.pallas_call(
+        fused,
+        out_shape=jax.ShapeDtypeStruct(latent.shape, BF16),
+        in_specs=[anywhere, vmem, anywhere, vmem, vmem, anywhere, vmem],
+        out_specs=vmem,
+        scratch_shapes=[
+            pltpu.VMEM((18, zs, 2, depth, chans), BF16),
+            pltpu.VMEM((frames + 2, rows + 2, across, chans), BF16),
+            pltpu.VMEM((frames + 2, rows + 2, across, chans), BF16),
+            pltpu.VMEM((frames + 2, rows + 2, across, 3 * chans), BF16),
+            pltpu.VMEM((frames, rows, across, chans), F32),
+            pltpu.SemaphoreType.DMA((UNITS,)),
+            pltpu.SemaphoreType.DMA,
+            pltpu.SemaphoreType.DMA((UNITS, 2, zs - 1)),
+            pltpu.SemaphoreType.DMA((UNITS, 2, zs - 1)),
+            pltpu.SemaphoreType.DMA((UNITS, 2, zs - 1)),
+            pltpu.SemaphoreType.DMA((UNITS, 2, zs - 1)),
+            pltpu.SemaphoreType.DMA((UNITS,)),
+            pltpu.SemaphoreType.DMA((UNITS,)),
+            pltpu.SemaphoreType.DMA((2, 3)),
+            pltpu.SemaphoreType.DMA((2, 3)),
+        ],
+        compiler_params=pltpu.CompilerParams(
+            collective_id=0, has_side_effects=True, vmem_limit_bytes=52 * 1024 * 1024
+        ),
+        cost_estimate=pl.CostEstimate(
+            flops=4 * frames * rows * across * 27 * chans * chans,
+            bytes_accessed=4 * 9 * depth * chans + 4 * frames * rows * across * chans,
+            transcendentals=0,
+        ),
+    )(latent, line(gain_first), flat(weight_first), line(bias_first), line(gain_second), flat(weight_second), line(bias_second))
+
+
 def solution(mesh):
+    small = mesh.shape["tile"] == 4 and mesh.shape["group"] == 8
     return jax.shard_map(
-        local,
+        fused_local if small else local,
         mesh=mesh,
         in_specs=(
             P(("cand", "group"), "tile", None, None),

time: 191 us -> 97.3 us (0.51); the launches traced: 189 us -> 97 us
  waiting for transfers between devices: 122 us -> 0 us
  Pallas kernels: 0 us -> 91.2 us
  matrix products: 23.5 us -> 0 us
  between operations: 13.8 us -> 0.02 us
  starting transfers between devices: 13.4 us -> 0 us
  local copies, waits for them, and re-layouts: 12.4 us -> 5.71 us
  other arithmetic: 3.79 us -> 0 us
    all_gather x2 -> x0, waiting for transfers between devices: 104 us -> none  [the longest x1 57.4 us: local(): lax.all_gather(weight_first, 'group', axis=2, tiled=True)]
    pallas_call x0 -> x1, Pallas kernels: none -> 91.2 us  [fused_local(): pl.pallas_call(fused, out_shape=jax.ShapeDtypeStruct(latent.shape, BF16),...]
    dot_general x18 -> x0, matrix products: 23.5 us -> none  [taps(): jnp.dot(window, piece[step_t, step_r], preferred_element_type=jnp.float32)]
    ppermute x6 -> x0, waiting for transfers between devices: 16.2 us -> none  [the longest x2 8.96 us: with_halo(): after = lax.ppermute(first, axis, down)]
    ppermute x6 -> x0, starting transfers between devices: 13.3 us -> none  [the longest x2 6.22 us: with_halo(): before = lax.ppermute(last, axis, up)]
    slice x6 -> x0, local copies, waits for them, and re-layouts: 8.56 us -> none  [the longest x2 7.24 us: taps(): joined[step_t:step_t + count, step_r:step_r + tall].reshape(-1, inner)]
    unnamed x38 -> x13, local copies, waits for them, and re-layouts: 3.71 us -> 5.7 us
    concatenate x4 -> x0, other arithmetic: 1.95 us -> none  [the longest x2 1.23 us: with_halo(): array = jnp.concatenate([before, array, after], axis=dim)]
  transfers between devices with their start and end apart: 8 -> 0, of which waited for: 8 -> 0; matrix products, arithmetic and copies ran while one was open for 12% -> 0% of each run, Pallas kernels for 0% -> 0%
where the time goes in v1:
time: 97.3 us; the launch traced here: 97 us
  Pallas kernels  91.2 us (94%)
  local copies, waits for them, and re-layouts  5.71 us (6%)
    pallas_call x1, Pallas kernels, fused_local(): pl.pallas_call(fused, out_shape=jax.ShapeDtypeStruct(latent.shape, BF16),...  91.2 us
    unnamed x13, local copies, waits for them, and re-layouts  5.7 us

profile of v1, /device:TPU:27, one launch (start us, length us, event | category | flops | bytes accessed | tf_op | source)
XLA Modules:
  0.0 97.0 jit_solution(5103762759541718500)
XLA Ops:
  0.0 0.0 copy-start.2
  0.0 0.7 copy-done.2
  0.7 0.0 copy-start.3
  0.7 0.7 copy-done.3
  1.4 0.0 copy-start.4
  1.4 0.7 copy-done.4
  2.0 0.0 copy-start.5
  2.1 0.7 copy-done.5
  2.7 0.0 copy-start
  2.7 1.2 %copy-done = bf16[3,3,144,384]{3,2,1,0:T(8,128)(2,1)S(1)} copy-done((bf16[3,3,144,384]{3,2,1,0:T(8,128)(2,1)S(1)}, bf16[3,3,144,384]{3,2,1,0:T(8,128)(2,1)}, u32[]{:S(2)}) %copy-start) | copy-done | bytes 995352
  3.9 0.0 copy-start.1
  3.9 1.0 %copy-done.1 = bf16[4,3,48,384]{3,2,1,0:T(8,128)(2,1)S(1)} copy-done((bf16[4,3,48,384]{3,2,1,0:T(8,128)(2,1)S(1)}, bf16[4,3,48,384]{3,2,1,0:T(8,128)(2,1)}, u32[]{:S(2)}) %copy-start.1) | copy-done | bytes 442392
  5.0 91.2 %shard_map.73 = bf16[4,3,48,384]{3,2,1,0:T(8,128)(2,1)S(1)} custom-call(bf16[4,3,48,384]{3,2,1,0:T(8,128)(2,1)S(1)} %copy-done.1, f32[1,384]{1,0:T(1,128)S(1)} %reshape.18.gain_first, bf16[9,144,384]{2,1,0:T(8,128)(2,1)S(1)} %bitcast.2, f32[1,384]{1,0:T(1,128)S(1)} %reshape.20.bias_first, f32[1,384]{1,0:T(1,128)S(1)} %reshape.21.gain_second, ...), custom_call_target="tpu_custom_call" | custom-call | flops 9172942848 | bytes 2875392 | tf_op jit(solution)/shard_map/pallas_call | solution.py:414
  96.2 0.8 copy.9
  (4 shorter events, 0.0 us)
Async XLA Ops:
  0.0 0.7 copy-start.2
  0.7 0.7 copy-start.3
  1.4 0.7 copy-start.4
  2.0 0.7 copy-start.5
  2.7 1.2 %copy-start = (bf16[3,3,144,384]{3,2,1,0:T(8,128)(2,1)S(1)}, bf16[3,3,144,384]{3,2,1,0:T(8,128)(2,1)}, u32[]{:S(2)}) copy-start(bf16[3,3,144,384]{3,2,1,0:T(8,128)(2,1)} %param.9) | copy-start | bytes 2985988
  3.9 1.0 %copy-start.1 = (bf16[4,3,48,384]{3,2,1,0:T(8,128)(2,1)S(1)}, bf16[4,3,48,384]{3,2,1,0:T(8,128)(2,1)}, u32[]{:S(2)}) copy-start(bf16[4,3,48,384]{3,2,1,0:T(8,128)(2,1)} %latent.1) | copy-start | bytes 1327108

commit v2 on v1

--- a/solution.py
+++ b/solution.py
@@ -76,7 +76,9 @@
 
 BF16, F32 = jnp.bfloat16, jnp.float32
 MESH = pl.DeviceIdType.MESH
-UNITS = 6
+UNITS = 18
+AHEAD = 3
+LAG = 2
 
 
 def act_slab(wide, gain):
@@ -86,9 +88,9 @@
 
 
 def fused(
-    latent, gain_first, weight_first, bias_first, gain_second, weight_second, bias_second, out,
-    taps_all, lat, sec, cols, total,
-    load_sem, lat_sem, z_send, z_recv, xy_send, xy_recv, core_send, core_recv, halo_send, halo_recv,
+    latent, gain_first_in, weight_first, bias_first_in, gain_second_in, weight_second, bias_second_in, out,
+    taps_all, lat, sec, cols, total, gain_first, bias_first, gain_second, bias_second,
+    load_sem, lat_sem, line_sem, z_send, z_recv, xy_send, xy_recv, core_send, core_recv, halo_send, halo_recv,
 ):
     tile, group = lax.axis_index("tile"), lax.axis_index("group")
     tiles, groups = lax.axis_size("tile"), lax.axis_size("group")
@@ -106,20 +108,36 @@
     sec[...] = jnp.zeros_like(sec)
     total[...] = jnp.zeros_like(total)
 
-    def load(unit):
-        source = weight_first if unit < 3 else weight_second
+
+    def load(at):
+        source, low, count, start = ((weight_first, 0, 1, 0), (weight_first, 1, 8, 1), (weight_second, 0, 9, 9))[at]
         return pltpu.make_async_copy(
-            source.at[pl.ds(3 * (unit % 3), 3)],
-            taps_all.at[pl.ds(3 * unit, 3), z, core],
-            load_sem.at[unit],
-        )
+            source.at[pl.ds(low, count)],
+            taps_all.at[pl.ds(start, count), z, pl.ds(3 * core, 3)],
+            load_sem.at[at],
+        )
+
+    line_copies = [
+        pltpu.make_async_copy(source, line, line_sem.at[at])
+        for at, (source, line) in enumerate(
+            (
+                (gain_first_in, gain_first),
+                (bias_first_in, bias_first),
+                (gain_second_in, gain_second),
+                (bias_second_in, bias_second),
+            )
+        )
+    ]
 
     lat_copy = pltpu.make_async_copy(
         latent, lat.at[pl.ds(2, frames), pl.ds(1, rows)], lat_sem
     )
-    for unit in range(UNITS):
-        load(unit).start()
+    load(0).start()
     lat_copy.start()
+    load(1).start()
+    load(2).start()
+    for copy in line_copies:
+        copy.start()
 
     barrier = pltpu.get_barrier_semaphore()
     partners = [
@@ -145,26 +163,30 @@
     pl.semaphore_wait(barrier, expected)
 
     def piece(unit, part, origin, where, send, recv):
-        block = taps_all.at[3 * unit + part, origin, core]
+        block = taps_all.at[unit, origin, 3 * core + part]
         return pltpu.make_async_remote_copy(
             src_ref=block, dst_ref=block, send_sem=send, recv_sem=recv,
             device_id=where, device_id_type=MESH,
         )
 
     def up(unit, dist):
-        return piece(unit, z_part, z - dist, {"group": group + 2}, z_send.at[unit, 0, dist], z_recv.at[unit, 0, dist])
+        return piece(unit, z_part, z - dist, {"group": group + 2}, z_send.at[unit], z_recv.at[unit, 0, dist])
 
     def down(unit, dist):
-        return piece(unit, z_part, z + dist, {"group": group - 2}, z_send.at[unit, 1, dist], z_recv.at[unit, 1, dist])
+        return piece(unit, z_part, z + dist, {"group": group - 2}, z_send.at[unit], z_recv.at[unit, 1, dist])
 
     def along_x(unit, step):
-        return piece(unit, x_part, (z + step) % zs, {"tile": x_tile}, xy_send.at[unit, 0, step - 1], xy_recv.at[unit, 0, step - 1])
+        return piece(unit, x_part, (z + step) % zs, {"tile": x_tile}, xy_send.at[unit], xy_recv.at[unit, 0])
 
     def along_y(unit, step):
-        return piece(unit, y_part, (z + step) % zs, {"tile": y_tile}, xy_send.at[unit, 1, step - 1], xy_recv.at[unit, 1, step - 1])
+        return piece(unit, y_part, (z + step) % zs, {"tile": y_tile}, xy_send.at[unit], xy_recv.at[unit, 1])
+
+    def wait_pieces(count, sem):
+        block = taps_all.at[0, 0, pl.ds(0, count)]
+        pltpu.make_async_copy(block, block, sem).wait()
 
     def across_cores(unit):
-        block = taps_all.at[pl.ds(3 * unit, 3), :, core]
+        block = taps_all.at[unit, :, pl.ds(3 * core, 3)]
         return pltpu.make_async_remote_copy(
             src_ref=block, dst_ref=block, send_sem=core_send.at[unit], recv_sem=core_recv.at[unit],
             device_id={"group": 2 * z + (1 - core)}, device_id_type=MESH,
@@ -257,15 +279,15 @@
     def first_columns():
         def step(frame, carry):
             for row in range(rows + 2):
-                spread(frame, row, act_slab(lat[frame, row].astype(F32), gain_first[...]))
+                spread(frame, row, act_slab(lat[frame, row].astype(F32), gain_first[...][None]))
             return carry
         lax.fori_loop(0, frames + 2, step, 0)
 
     def second_values():
         def step(frame, carry):
             for row in range(rows):
-                hidden = total[frame, row] + bias_first[...]
-                sec[frame + 2, row + 1] = act_slab(hidden, gain_second[...]).astype(BF16)
+                hidden = total[frame, row] + bias_first[...][None]
+                sec[frame + 2, row + 1] = act_slab(hidden, gain_second[...][None]).astype(BF16)
             return carry
         lax.fori_loop(0, frames, step, 0)
         total[...] = jnp.zeros_like(total)
@@ -278,22 +300,22 @@
         lax.fori_loop(0, frames + 2, step, 0)
 
     def multiply(unit):
-        step_t = unit % 3
-
-        def step(step_r, carry):
-            window = cols[pl.ds(step_t, frames), pl.ds(step_r, rows)].reshape(-1, 3 * chans)
-            weight = taps_all[3 * unit + step_r].reshape(3 * chans, chans)
-            added = jnp.dot(window, weight, preferred_element_type=F32)
-            total[...] += added.reshape(frames, rows, across, chans)
-            return carry
-        lax.fori_loop(0, 3, step, 0)
+        step_t, step_r = (unit % 9) // 3, unit % 3
+        window = cols[pl.ds(step_t, frames), pl.ds(step_r, rows)].reshape(-1, 3 * chans)
+        weight = taps_all[unit].reshape(3 * chans, chans)
+        added = jnp.dot(window, weight, preferred_element_type=F32)
+        total[...] += added.reshape(frames, rows, across, chans)
 
     load(0).wait()
     own(0)
     lat_copy.wait()
+    load(1).wait()
+    for unit in range(1, AHEAD):
+        own(unit)
     send_frames(lat, 0)
-    for unit in range(1, UNITS):
-        load(unit).wait()
+    load(2).wait()
+    for copy in line_copies:
+        copy.wait()
 
     def stage(index, lag, body):
         unit = index - lag
@@ -303,94 +325,105 @@
             body(unit)
 
     def direct(unit):
-        for step in range(1, zs):
-            @pl.when(tile != 2)
-            def _():
-                along_x(unit, step).wait_recv()
-
-            @pl.when(tile != 1)
-            def _():
-                along_y(unit, step).wait_recv()
-
-            @pl.when(corner)
-            def _():
+        @pl.when(tile != 2)
+        def _():
+            wait_pieces(3, xy_recv.at[unit, 0])
+
+        @pl.when(tile != 1)
+        def _():
+            wait_pieces(3, xy_recv.at[unit, 1])
+
+        @pl.when(corner)
+        def _():
+            for step in range(1, zs):
                 along_x(unit, step).start()
                 along_y(unit, step).start()
 
     def forwarded(unit):
-        for step in range(1, zs):
-            @pl.when(tile == 2)
-            def _():
-                along_x(unit, step).wait_recv()
-
-            @pl.when(tile == 1)
-            def _():
-                along_y(unit, step).wait_recv()
+        @pl.when(tile == 2)
+        def _():
+            wait_pieces(3, xy_recv.at[unit, 0])
+
+        @pl.when(tile == 1)
+        def _():
+            wait_pieces(3, xy_recv.at[unit, 1])
         across_cores(unit).start()
 
-    def compute(unit):
+    def compute(unit, carry):
         across_cores(unit).wait_recv()
         multiply(unit)
-
-    lag = zs + 1
+        return carry
+
+    def drain(unit):
+        @pl.when((z > 0) & (z < zs - 1))
+        def _():
+            wait_pieces(zs + 1, z_send.at[unit])
+
+        @pl.when((z == 0) | (z == zs - 1))
+        def _():
+            wait_pieces(1, z_send.at[unit])
+        wait_pieces(2 * zs - 2, xy_send.at[unit])
+        across_cores(unit).wait_send()
+
+    half = UNITS // 2
+    direct_lag = LAG * (zs - 1)
+    forward_lag = direct_lag + LAG
+    first_lag = forward_lag + LAG
+    middle = half - 1 + first_lag
+    drain_lag = first_lag + 4
+    turns = UNITS + forward_lag + 1
+
+    def done_by(index):
+        first = jnp.clip(index - first_lag + 1, 0, half)
+        second = jnp.clip(jnp.minimum(2 * (index - middle - 2), index - forward_lag - half), 0, half)
+        return first + second
+
     def turn(index, carry):
-        stage(index, -1, own)
+        stage(index, -AHEAD, own)
         for dist in range(1, zs):
-            stage(index, dist - 1, lambda unit: arrived(unit, dist))
-
-        @pl.when(index == 0)
+            stage(index, LAG * (dist - 1), lambda unit: arrived(unit, dist))
+        stage(index, direct_lag, direct)
+        stage(index, forward_lag, forwarded)
+        stage(index, drain_lag, drain)
+        lax.fori_loop(done_by(index - 1), done_by(index), compute, 0)
+
+        @pl.when(index == 1)
         def _():
             send_rows(lat, 0)
 
-        @pl.when(index == 2)
+        @pl.when(index == 3)
         def _():
             await_rows(lat, 0)
             first_columns()
 
-        @pl.when(index == lag + 3)
+        @pl.when(index == middle)
+        def _():
+            second_values()
+            send_frames(sec, 1)
+
+        @pl.when(index == middle + 1)
         def _():
             send_rows(sec, 1)
 
-        stage(index, zs - 1, direct)
-        stage(index, zs, forwarded)
-
-        @pl.when(index == lag + 3)
+        @pl.when(index == middle + 2)
         def _():
             await_rows(sec, 1)
             second_columns()
-
-        stage(index, lag, compute)
-
-        @pl.when(index == lag + 2)
-        def _():
-            second_values()
-            send_frames(sec, 1)
         return carry
 
-    lax.fori_loop(0, UNITS + lag, turn, 0)
+    lax.fori_loop(0, turns, turn, 0)
 
     def finish(frame, carry):
         for row in range(rows):
-            value = lat[frame + 2, row + 1].astype(F32) + total[frame, row] + bias_second[...]
+            value = lat[frame + 2, row + 1].astype(F32) + total[frame, row] + bias_second[...][None]
             out[frame, row] = value.astype(BF16)
         return carry
     lax.fori_loop(0, frames, finish, 0)
 
-    def drain(unit, carry):
-        for dist in range(zs - 1):
-            @pl.when((z >= dist) & (z < zs - 1))
-            def _():
-                up(unit, dist).wait_send()
-
-            @pl.when((z + dist < zs) & (z > 0))
-            def _():
-                down(unit, dist).wait_send()
-        for step in range(1, zs):
-            along_x(unit, step).wait_send()
-            along_y(unit, step).wait_send()
-        across_cores(unit).wait_send()
+    def drain_rest(unit, carry):
+        drain(unit)
         return carry
-    lax.fori_loop(0, UNITS, drain, 0)
+    lax.fori_loop(turns - drain_lag, UNITS, drain_rest, 0)
     for which, buf in enumerate((lat, sec)):
         @pl.when(group < groups - 1)
         def _():
@@ -408,40 +441,41 @@
 def fused_local(latent, gain_first, weight_first, bias_first, gain_second, weight_second, bias_second):
     frames, rows, across, chans = latent.shape
     depth, zs = weight_first.shape[2], lax.axis_size("group") // 2
-    line = lambda values: values.reshape(1, chans)
-    flat = lambda weight: weight.reshape(9, depth, chans)
-    vmem, anywhere = pl.BlockSpec(memory_space=pltpu.VMEM), pl.BlockSpec(memory_space=pl.ANY)
+    flat = lambda weight: weight.reshape(9, 3, depth // 3, chans)
+    anywhere = pl.BlockSpec(memory_space=pl.ANY)
     return pl.pallas_call(
         fused,
         out_shape=jax.ShapeDtypeStruct(latent.shape, BF16),
-        in_specs=[anywhere, vmem, anywhere, vmem, vmem, anywhere, vmem],
-        out_specs=vmem,
+        in_specs=[anywhere] * 7,
+        out_specs=pl.BlockSpec(memory_space=pltpu.VMEM),
         scratch_shapes=[
-            pltpu.VMEM((18, zs, 2, depth, chans), BF16),
+            pltpu.VMEM((UNITS, zs, 6, depth // 3, chans), BF16),
             pltpu.VMEM((frames + 2, rows + 2, across, chans), BF16),
             pltpu.VMEM((frames + 2, rows + 2, across, chans), BF16),
             pltpu.VMEM((frames + 2, rows + 2, across, 3 * chans), BF16),
             pltpu.VMEM((frames, rows, across, chans), F32),
+            *[pltpu.VMEM((chans,), F32)] * 4,
+            pltpu.SemaphoreType.DMA((3,)),
+            pltpu.SemaphoreType.DMA,
+            pltpu.SemaphoreType.DMA((4,)),
             pltpu.SemaphoreType.DMA((UNITS,)),
-            pltpu.SemaphoreType.DMA,
             pltpu.SemaphoreType.DMA((UNITS, 2, zs - 1)),
-            pltpu.SemaphoreType.DMA((UNITS, 2, zs - 1)),
-            pltpu.SemaphoreType.DMA((UNITS, 2, zs - 1)),
-            pltpu.SemaphoreType.DMA((UNITS, 2, zs - 1)),
+            pltpu.SemaphoreType.DMA((UNITS,)),
+            pltpu.SemaphoreType.DMA((UNITS, 2)),
             pltpu.SemaphoreType.DMA((UNITS,)),
             pltpu.SemaphoreType.DMA((UNITS,)),
             pltpu.SemaphoreType.DMA((2, 3)),
             pltpu.SemaphoreType.DMA((2, 3)),
         ],
         compiler_params=pltpu.CompilerParams(
-            collective_id=0, has_side_effects=True, vmem_limit_bytes=52 * 1024 * 1024
+            collective_id=0, has_side_effects=True, vmem_limit_bytes=60 * 1024 * 1024
         ),
         cost_estimate=pl.CostEstimate(
             flops=4 * frames * rows * across * 27 * chans * chans,
             bytes_accessed=4 * 9 * depth * chans + 4 * frames * rows * across * chans,
             transcendentals=0,
         ),
-    )(latent, line(gain_first), flat(weight_first), line(bias_first), line(gain_second), flat(weight_second), line(bias_second))
+    )(latent, gain_first, flat(weight_first), bias_first, gain_second, flat(weight_second), bias_second)
 
 
 def solution(mesh):

time: 97.3 us -> 87.1 us (0.90)
  the two profiles are of different devices: /device:TPU:27 before, /device:TPU:1 now
where the time goes in v2:
time: 87.1 us; the launch traced here: 86.9 us
  Pallas kernels  85.1 us (98%)
  local copies, waits for them, and re-layouts  1.82 us (2%)
    pallas_call x1, Pallas kernels, fused_local(): pl.pallas_call(fused, out_shape=jax.ShapeDtypeStruct(latent.shape, BF16),...  85.1 us
    unnamed x1, local copies, waits for them, and re-layouts  1.82 us

profile of v2, /device:TPU:1, one launch (start us, length us, event | category | flops | bytes accessed | tf_op | source)
XLA Modules:
  0.0 86.9 jit_solution(11832355750637898749)
XLA Ops:
  0.0 85.1 %shard_map.73 = bf16[4,3,48,384]{3,2,1,0:T(8,128)(2,1)} custom-call(bf16[4,3,48,384]{3,2,1,0:T(8,128)(2,1)} %latent.1, f32[384]{0:T(512)} %gain_first_in.1, bf16[9,3,48,384]{3,2,1,0:T(8,128)(2,1)} %bitcast.2, f32[384]{0:T(512)} %bias_first_in.1, f32[384]{0:T(512)} %gain_second_in.1, bf16[9,3,48,384]{3,2,1,0:T(8,128)(2,1)} %bitcast.3, f32[384]{0:T(512)} %bias_second_in.1), custom_call_target="tpu_custom_call" | custom-call | flops 9172942848 | bytes 2875392 | tf_op jit(solution)/shard_map/pallas_call | solution.py:446
  85.1 1.8 %copy.9 = bf16[4,3,48,384]{3,2,1,0:T(8,128)(2,1)} copy(bf16[4,3,48,384]{3,2,1,0:T(8,128)(2,1)} %shard_map.73) | data formatting | bytes 884736

commit v3 on v2

--- a/solution.py
+++ b/solution.py
@@ -77,8 +77,8 @@
 BF16, F32 = jnp.bfloat16, jnp.float32
 MESH = pl.DeviceIdType.MESH
 UNITS = 18
-AHEAD = 3
-LAG = 2
+AHEAD = 6
+LAG = 3
 
 
 def act_slab(wide, gain):

time: 87.1 us -> 94.2 us (1.082)
  the two profiles are of different devices: /device:TPU:1 before, /device:TPU:0 now
where the time goes in v3:
time: 94.2 us; the launch traced here: 94 us
  Pallas kernels  92.2 us (98%)
  local copies, waits for them, and re-layouts  1.82 us (2%)
    pallas_call x1, Pallas kernels, fused_local(): pl.pallas_call(fused, out_shape=jax.ShapeDtypeStruct(latent.shape, BF16),...  92.2 us

profile of v3, /device:TPU:0, one launch (start us, length us, event | category | flops | bytes accessed | tf_op | source)
XLA Modules:
  0.0 94.0 jit_solution(8944778718557448237)
XLA Ops:
  0.0 92.2 %shard_map.73 = bf16[4,3,48,384]{3,2,1,0:T(8,128)(2,1)} custom-call(bf16[4,3,48,384]{3,2,1,0:T(8,128)(2,1)} %latent.1, f32[384]{0:T(512)} %gain_first_in.1, bf16[9,3,48,384]{3,2,1,0:T(8,128)(2,1)} %bitcast.2, f32[384]{0:T(512)} %bias_first_in.1, f32[384]{0:T(512)} %gain_second_in.1, bf16[9,3,48,384]{3,2,1,0:T(8,128)(2,1)} %bitcast.3, f32[384]{0:T(512)} %bias_second_in.1), custom_call_target="tpu_custom_call" | custom-call | flops 9172942848 | bytes 2875392 | tf_op jit(solution)/shard_map/pallas_call | solution.py:446
  92.2 1.8 %copy.9 = bf16[4,3,48,384]{3,2,1,0:T(8,128)(2,1)} copy(bf16[4,3,48,384]{3,2,1,0:T(8,128)(2,1)} %shard_map.73) | data formatting | bytes 884736

commit v4 on v2

--- a/solution.py
+++ b/solution.py
@@ -78,7 +78,7 @@
 MESH = pl.DeviceIdType.MESH
 UNITS = 18
 AHEAD = 3
-LAG = 2
+LAG = 1
 
 
 def act_slab(wide, gain):

time: 87.1 us -> 97.7 us (1.12)
  the two profiles are of different devices: /device:TPU:1 before, /device:TPU:27 now
where the time goes in v4:
time: 97.7 us; the launch traced here: 97 us
  Pallas kernels  95.2 us (97%)
  local copies, waits for them, and re-layouts  1.82 us (2%)
    pallas_call x1, Pallas kernels, fused_local(): pl.pallas_call(fused, out_shape=jax.ShapeDtypeStruct(latent.shape, BF16),...  95.2 us

profile of v4, /device:TPU:27, one launch (start us, length us, event | category | flops | bytes accessed | tf_op | source)
XLA Modules:
  0.0 97.0 jit_solution(10348013994324079052)
XLA Ops:
  0.0 95.2 %shard_map.73 = bf16[4,3,48,384]{3,2,1,0:T(8,128)(2,1)} custom-call(bf16[4,3,48,384]{3,2,1,0:T(8,128)(2,1)} %latent.1, f32[384]{0:T(512)} %gain_first_in.1, bf16[9,3,48,384]{3,2,1,0:T(8,128)(2,1)} %bitcast.2, f32[384]{0:T(512)} %bias_first_in.1, f32[384]{0:T(512)} %gain_second_in.1, bf16[9,3,48,384]{3,2,1,0:T(8,128)(2,1)} %bitcast.3, f32[384]{0:T(512)} %bias_second_in.1), custom_call_target="tpu_custom_call" | custom-call | flops 9172942848 | bytes 2875392 | tf_op jit(solution)/shard_map/pallas_call | solution.py:446
  95.2 1.8 %copy.9 = bf16[4,3,48,384]{3,2,1,0:T(8,128)(2,1)} copy(bf16[4,3,48,384]{3,2,1,0:T(8,128)(2,1)} %shard_map.73) | data formatting | bytes 884736

commit v5 on v2

--- a/solution.py
+++ b/solution.py
@@ -143,6 +143,12 @@
     partners = [
         ({"group": group + 2}, z < zs - 1),
         ({"group": group - 2}, z > 0),
+        ({"group": group + 4}, z < zs - 2),
+        ({"group": group - 4}, z > 1),
+        ({"tile": tile + 1, "group": group + 1}, (tile < tiles - 1) & (group < groups - 1)),
+        ({"tile": tile - 1, "group": group + 1}, (tile > 0) & (group < groups - 1)),
+        ({"tile": tile + 1, "group": group - 1}, (tile < tiles - 1) & (group > 0)),
+        ({"tile": tile - 1, "group": group - 1}, (tile > 0) & (group > 0)),
         ({"group": group + 1}, group < groups - 1),
         ({"group": group - 1}, group > 0),
         ({"tile": tile + 1}, tile < tiles - 1),
@@ -169,17 +175,15 @@
             device_id=where, device_id_type=MESH,
         )
 
-    def up(unit, dist):
-        return piece(unit, z_part, z - dist, {"group": group + 2}, z_send.at[unit], z_recv.at[unit, 0, dist])
-
-    def down(unit, dist):
-        return piece(unit, z_part, z + dist, {"group": group - 2}, z_send.at[unit], z_recv.at[unit, 1, dist])
-
-    def along_x(unit, step):
-        return piece(unit, x_part, (z + step) % zs, {"tile": x_tile}, xy_send.at[unit], xy_recv.at[unit, 0])
-
-    def along_y(unit, step):
-        return piece(unit, y_part, (z + step) % zs, {"tile": y_tile}, xy_send.at[unit], xy_recv.at[unit, 1])
+    def along_z(unit, origin, delta):
+        slot = (origin - (z + delta) + zs) % zs - 1
+        return piece(unit, z_part, origin, {"group": group + 2 * delta}, z_send.at[unit], z_recv.at[unit, slot])
+
+    def along_x(unit, origin):
+        return piece(unit, x_part, origin, {"tile": x_tile}, xy_send.at[unit], xy_recv.at[unit, 0])
+
+    def along_y(unit, origin):
+        return piece(unit, y_part, origin, {"tile": y_tile}, xy_send.at[unit], xy_recv.at[unit, 1])
 
     def wait_pieces(count, sem):
         block = taps_all.at[0, 0, pl.ds(0, count)]
@@ -192,80 +196,80 @@
             device_id={"group": 2 * z + (1 - core)}, device_id_type=MESH,
         )
 
+    at_end = (z == 0) | (z == zs - 1)
+    low_side = (z < 2).astype(jnp.int32)
+    inward = 2 * low_side - 1
+
     def own(unit):
-        @pl.when(z < zs - 1)
-        def _():
-            up(unit, 0).start()
-
-        @pl.when(z > 0)
-        def _():
-            down(unit, 0).start()
-
-    def hand_on(unit, step):
+        along_z(unit, z, inward).start()
+
+        @pl.when(at_end)
+        def _():
+            along_z(unit, z, 2 * inward).start()
+
+        @pl.when(jnp.logical_not(at_end))
+        def _():
+            along_z(unit, z, -inward).start()
+
+    def hand_on(unit, origin):
         @pl.when(jnp.logical_not(corner))
         def _():
-            along_x(unit, step).start()
-            along_y(unit, step).start()
-
-    def arrived(unit, dist):
-        @pl.when(z >= dist)
-        def _():
-            up(unit, dist - 1).wait_recv()
-            if dist < zs - 1:
-                @pl.when(z < zs - 1)
-                def _():
-                    up(unit, dist).start()
-            hand_on(unit, zs - dist)
-
-        @pl.when(z + dist < zs)
-        def _():
-            down(unit, dist - 1).wait_recv()
-            if dist < zs - 1:
-                @pl.when(z > 0)
-                def _():
-                    down(unit, dist).start()
-            hand_on(unit, dist)
-
-    def frame_copy(buf, which):
-        return pltpu.make_async_remote_copy(
-            src_ref=buf.at[pl.ds(frames, 2), pl.ds(1, rows)], dst_ref=buf.at[pl.ds(0, 2), pl.ds(1, rows)],
-            send_sem=halo_send.at[which, 0], recv_sem=halo_recv.at[which, 0],
-            device_id={"group": group + 1}, device_id_type=MESH,
+            along_x(unit, origin).start()
+            along_y(unit, origin).start()
+
+    def await_z(unit, origin):
+        wait_pieces(1, z_recv.at[unit, (origin - z + zs) % zs - 1])
+
+    def near(unit):
+        @pl.when(at_end)
+        def _():
+            await_z(unit, z + inward)
+            hand_on(unit, z + inward)
+
+        @pl.when(jnp.logical_not(at_end))
+        def _():
+            await_z(unit, z + inward)
+            along_z(unit, z + inward, -inward).start()
+            hand_on(unit, z + inward)
+            await_z(unit, z - inward)
+            hand_on(unit, z - inward)
+            await_z(unit, z + 2 * inward)
+            along_z(unit, z + 2 * inward, -inward).start()
+            hand_on(unit, z + 2 * inward)
+
+    def far(unit):
+        @pl.when(at_end)
+        def _():
+            for steps in (2, 3):
+                await_z(unit, z + steps * inward)
+                hand_on(unit, z + steps * inward)
+
+    def halo_copies(buf, which):
+        late, low, high = pl.ds(frames, 2), tile > 0, tile < tiles - 1
+        sends, gets = group < groups - 1, group > 0
+        inner, body = pl.ds(1, rows), pl.ds(2, frames)
+        plan = (
+            ((late, inner), (pl.ds(0, 2), inner), {"group": group + 1}, sends, gets),
+            ((body, rows), (body, 0), {"tile": tile + 1}, high, low),
+            ((body, 1), (body, rows + 1), {"tile": tile - 1}, low, high),
+            ((late, rows), (pl.ds(0, 2), 0), {"tile": tile + 1, "group": group + 1}, sends & high, gets & low),
+            ((late, 1), (pl.ds(0, 2), rows + 1), {"tile": tile - 1, "group": group + 1}, sends & low, gets & high),
         )
-
-    def row_copy(buf, which, later):
-        return pltpu.make_async_remote_copy(
-            src_ref=buf.at[:, rows if later else 1], dst_ref=buf.at[:, 0 if later else rows + 1],
-            send_sem=halo_send.at[which, 1 + later], recv_sem=halo_recv.at[which, 1 + later],
-            device_id={"tile": tile + 1 if later else tile - 1}, device_id_type=MESH,
-        )
-
-    def send_frames(buf, which):
-        @pl.when(group < groups - 1)
-        def _():
-            frame_copy(buf, which).start()
-
-    def send_rows(buf, which):
-        @pl.when(group > 0)
-        def _():
-            frame_copy(buf, which).wait_recv()
-
-        @pl.when(tile < tiles - 1)
-        def _():
-            row_copy(buf, which, 1).start()
-
-        @pl.when(tile > 0)
-        def _():
-            row_copy(buf, which, 0).start()
-
-    def await_rows(buf, which):
-        @pl.when(tile > 0)
-        def _():
-            row_copy(buf, which, 1).wait_recv()
-
-        @pl.when(tile < tiles - 1)
-        def _():
-            row_copy(buf, which, 0).wait_recv()
+        for at, (source, target, where, there, here) in enumerate(plan):
+            copy = pltpu.make_async_remote_copy(
+                src_ref=buf.at[source], dst_ref=buf.at[target],
+                send_sem=halo_send.at[which, at], recv_sem=halo_recv.at[which, at],
+                device_id=where, device_id_type=MESH,
+            )
+            yield copy, there, here
+
+    def send_halo(buf, which):
+        for copy, there, _ in halo_copies(buf, which):
+            pl.when(there)(copy.start)
+
+    def await_halo(buf, which):
+        for copy, _, here in halo_copies(buf, which):
+            pl.when(here)(copy.wait_recv)
 
     column = lax.broadcasted_iota(jnp.int32, (across, chans), 0)
 
@@ -312,7 +316,7 @@
     load(1).wait()
     for unit in range(1, AHEAD):
         own(unit)
-    send_frames(lat, 0)
+    send_halo(lat, 0)
     load(2).wait()
     for copy in line_copies:
         copy.wait()
@@ -336,8 +340,8 @@
         @pl.when(corner)
         def _():
             for step in range(1, zs):
-                along_x(unit, step).start()
-                along_y(unit, step).start()
+                along_x(unit, (z + step) % zs).start()
+                along_y(unit, (z + step) % zs).start()
 
     def forwarded(unit):
         @pl.when(tile == 2)
@@ -355,59 +359,51 @@
         return carry
 
     def drain(unit):
-        @pl.when((z > 0) & (z < zs - 1))
-        def _():
-            wait_pieces(zs + 1, z_send.at[unit])
-
-        @pl.when((z == 0) | (z == zs - 1))
-        def _():
-            wait_pieces(1, z_send.at[unit])
+        @pl.when(at_end)
+        def _():
+            wait_pieces(2, z_send.at[unit])
+
+        @pl.when(jnp.logical_not(at_end))
+        def _():
+            wait_pieces(4, z_send.at[unit])
         wait_pieces(2 * zs - 2, xy_send.at[unit])
         across_cores(unit).wait_send()
 
     half = UNITS // 2
-    direct_lag = LAG * (zs - 1)
+    direct_lag = 2 * LAG
     forward_lag = direct_lag + LAG
-    first_lag = forward_lag + LAG
+    first_lag = forward_lag + 1
     middle = half - 1 + first_lag
     drain_lag = first_lag + 4
-    turns = UNITS + forward_lag + 1
+    turns = UNITS + first_lag
 
     def done_by(index):
         first = jnp.clip(index - first_lag + 1, 0, half)
-        second = jnp.clip(jnp.minimum(2 * (index - middle - 2), index - forward_lag - half), 0, half)
+        second = jnp.clip(jnp.minimum(2 * (index - middle - 1), index - first_lag - half + 1), 0, half)
         return first + second
 
     def turn(index, carry):
         stage(index, -AHEAD, own)
-        for dist in range(1, zs):
-            stage(index, LAG * (dist - 1), lambda unit: arrived(unit, dist))
+        stage(index, 0, near)
+        stage(index, LAG, far)
         stage(index, direct_lag, direct)
         stage(index, forward_lag, forwarded)
         stage(index, drain_lag, drain)
         lax.fori_loop(done_by(index - 1), done_by(index), compute, 0)
 
-        @pl.when(index == 1)
-        def _():
-            send_rows(lat, 0)
-
-        @pl.when(index == 3)
-        def _():
-            await_rows(lat, 0)
+        @pl.when(index == 2)
+        def _():
+            await_halo(lat, 0)
             first_columns()
 
         @pl.when(index == middle)
         def _():
             second_values()
-            send_frames(sec, 1)
+            send_halo(sec, 1)
 
         @pl.when(index == middle + 1)
         def _():
-            send_rows(sec, 1)
-
-        @pl.when(index == middle + 2)
-        def _():
-            await_rows(sec, 1)
+            await_halo(sec, 1)
             second_columns()
         return carry
 
@@ -425,17 +421,8 @@
         return carry
     lax.fori_loop(turns - drain_lag, UNITS, drain_rest, 0)
     for which, buf in enumerate((lat, sec)):
-        @pl.when(group < groups - 1)
-        def _():
-            frame_copy(buf, which).wait_send()
-
-        @pl.when(tile < tiles - 1)
-        def _():
-            row_copy(buf, which, 1).wait_send()
-
-        @pl.when(tile > 0)
-        def _():
-            row_copy(buf, which, 0).wait_send()
+        for copy, there, _ in halo_copies(buf, which):
+            pl.when(there)(copy.wait_send)
 
 
 def fused_local(latent, gain_first, weight_first, bias_first, gain_second, weight_second, bias_second):
@@ -459,13 +446,13 @@
             pltpu.SemaphoreType.DMA,
             pltpu.SemaphoreType.DMA((4,)),
             pltpu.SemaphoreType.DMA((UNITS,)),
-            pltpu.SemaphoreType.DMA((UNITS, 2, zs - 1)),
+            pltpu.SemaphoreType.DMA((UNITS, zs - 1)),
             pltpu.SemaphoreType.DMA((UNITS,)),
             pltpu.SemaphoreType.DMA((UNITS, 2)),
             pltpu.SemaphoreType.DMA((UNITS,)),
             pltpu.SemaphoreType.DMA((UNITS,)),
-            pltpu.SemaphoreType.DMA((2, 3)),
-            pltpu.SemaphoreType.DMA((2, 3)),
+            pltpu.SemaphoreType.DMA((2, 5)),
+            pltpu.SemaphoreType.DMA((2, 5)),
         ],
         compiler_params=pltpu.CompilerParams(
             collective_id=0, has_side_effects=True, vmem_limit_bytes=60 * 1024 * 1024

time: 87.1 us -> 82.2 us (0.944)
  the two profiles are of different devices: /device:TPU:1 before, /device:TPU:11 now
where the time goes in v5:
time: 82.2 us; the launch traced here: 82 us
  Pallas kernels  80.2 us (98%)
  local copies, waits for them, and re-layouts  1.82 us (2%)
    pallas_call x1, Pallas kernels, fused_local(): pl.pallas_call(fused, out_shape=jax.ShapeDtypeStruct(latent.shape, BF16),...  80.2 us
    unnamed x1, local copies, waits for them, and re-layouts  1.82 us

profile of v5, /device:TPU:11, one launch (start us, length us, event | category | flops | bytes accessed | tf_op | source)
XLA Modules:
  0.0 82.0 jit_solution(18193471262170734549)
XLA Ops:
  0.0 80.2 %shard_map.73 = bf16[4,3,48,384]{3,2,1,0:T(8,128)(2,1)} custom-call(bf16[4,3,48,384]{3,2,1,0:T(8,128)(2,1)} %latent.1, f32[384]{0:T(512)} %gain_first_in.1, bf16[9,3,48,384]{3,2,1,0:T(8,128)(2,1)} %bitcast.2, f32[384]{0:T(512)} %bias_first_in.1, f32[384]{0:T(512)} %gain_second_in.1, bf16[9,3,48,384]{3,2,1,0:T(8,128)(2,1)} %bitcast.3, f32[384]{0:T(512)} %bias_second_in.1), custom_call_target="tpu_custom_call" | custom-call | flops 9172942848 | bytes 2875392 | tf_op jit(solution)/shard_map/pallas_call | solution.py:433
  80.2 1.8 %copy.9 = bf16[4,3,48,384]{3,2,1,0:T(8,128)(2,1)} copy(bf16[4,3,48,384]{3,2,1,0:T(8,128)(2,1)} %shard_map.73) | data formatting | bytes 884736

commit v6 on v5

--- a/solution.py
+++ b/solution.py
@@ -106,7 +106,6 @@
 
     lat[...] = jnp.zeros_like(lat)
     sec[...] = jnp.zeros_like(sec)
-    total[...] = jnp.zeros_like(total)
 
 
     def load(at):
@@ -280,12 +279,9 @@
         cols[frame, row, :, chans : 2 * chans] = value.astype(BF16)
         cols[frame, row, :, 2 * chans : 3 * chans] = after.astype(BF16)
 
-    def first_columns():
-        def step(frame, carry):
-            for row in range(rows + 2):
-                spread(frame, row, act_slab(lat[frame, row].astype(F32), gain_first[...][None]))
-            return carry
-        lax.fori_loop(0, frames + 2, step, 0)
+    def first_columns(frame):
+        for row in range(rows + 2):
+            spread(frame, row, act_slab(lat[frame, row].astype(F32), gain_first[...][None]))
 
     def second_values():
         def step(frame, carry):
@@ -296,12 +292,12 @@
         lax.fori_loop(0, frames, step, 0)
         total[...] = jnp.zeros_like(total)
 
-    def second_columns():
+    def second_columns(low, high, chosen):
         def step(frame, carry):
-            for row in range(rows + 2):
+            for row in chosen:
                 spread(frame, row, sec[frame, row].astype(F32))
             return carry
-        lax.fori_loop(0, frames + 2, step, 0)
+        lax.fori_loop(low, high, step, 0)
 
     def multiply(unit):
         step_t, step_r = (unit % 9) // 3, unit % 3
@@ -317,6 +313,7 @@
     for unit in range(1, AHEAD):
         own(unit)
     send_halo(lat, 0)
+    total[...] = jnp.zeros_like(total)
     load(2).wait()
     for copy in line_copies:
         copy.wait()
@@ -373,13 +370,14 @@
     direct_lag = 2 * LAG
     forward_lag = direct_lag + LAG
     first_lag = forward_lag + 1
+    assert frames + 2 < first_lag
     middle = half - 1 + first_lag
     drain_lag = first_lag + 4
     turns = UNITS + first_lag
 
     def done_by(index):
         first = jnp.clip(index - first_lag + 1, 0, half)
-        second = jnp.clip(jnp.minimum(2 * (index - middle - 1), index - first_lag - half + 1), 0, half)
+        second = jnp.clip(jnp.minimum(2 * (index - middle - 2), index - first_lag - half + 1), 0, half)
         return first + second
 
     def turn(index, carry):
@@ -391,10 +389,13 @@
         stage(index, drain_lag, drain)
         lax.fori_loop(done_by(index - 1), done_by(index), compute, 0)
 
-        @pl.when(index == 2)
+        @pl.when(index == 1)
         def _():
             await_halo(lat, 0)
-            first_columns()
+
+        @pl.when((index >= 1) & (index < frames + 3))
+        def _():
+            first_columns(index - 1)
 
         @pl.when(index == middle)
         def _():
@@ -403,8 +404,13 @@
 
         @pl.when(index == middle + 1)
         def _():
+            second_columns(2, frames + 2, range(1, rows + 1))
+
+        @pl.when(index == middle + 2)
+        def _():
             await_halo(sec, 1)
-            second_columns()
+            second_columns(0, 2, range(rows + 2))
+            second_columns(2, frames + 2, (0, rows + 1))
         return carry
 
     lax.fori_loop(0, turns, turn, 0)

time: 82.2 us -> 80.2 us (0.976)
  the two profiles are of different devices: /device:TPU:11 before, /device:TPU:27 now
where the time goes in v6:
time: 80.2 us; the launch traced here: 79.1 us
  Pallas kernels  77.3 us (96%)
  local copies, waits for them, and re-layouts  1.82 us (2%)
    pallas_call x1, Pallas kernels, fused_local(): pl.pallas_call(fused, out_shape=jax.ShapeDtypeStruct(latent.shape, BF16),...  77.3 us
    unnamed x1, local copies, waits for them, and re-layouts  1.82 us

profile of v6, /device:TPU:27, one launch (start us, length us, event | category | flops | bytes accessed | tf_op | source)
XLA Modules:
  0.0 79.1 jit_solution(2444105663537704838)
XLA Ops:
  0.0 77.3 %shard_map.73 = bf16[4,3,48,384]{3,2,1,0:T(8,128)(2,1)} custom-call(bf16[4,3,48,384]{3,2,1,0:T(8,128)(2,1)} %latent.1, f32[384]{0:T(512)} %gain_first_in.1, bf16[9,3,48,384]{3,2,1,0:T(8,128)(2,1)} %bitcast.2, f32[384]{0:T(512)} %bias_first_in.1, f32[384]{0:T(512)} %gain_second_in.1, bf16[9,3,48,384]{3,2,1,0:T(8,128)(2,1)} %bitcast.3, f32[384]{0:T(512)} %bias_second_in.1), custom_call_target="tpu_custom_call" | custom-call | flops 9172942848 | bytes 2875392 | tf_op jit(solution)/shard_map/pallas_call | solution.py:439
  77.3 1.8 %copy.9 = bf16[4,3,48,384]{3,2,1,0:T(8,128)(2,1)} copy(bf16[4,3,48,384]{3,2,1,0:T(8,128)(2,1)} %shard_map.73) | data formatting | bytes 884736

commit v7 on v6

--- a/solution.py
+++ b/solution.py
@@ -109,10 +109,10 @@
 
 
     def load(at):
-        source, low, count, start = ((weight_first, 0, 1, 0), (weight_first, 1, 8, 1), (weight_second, 0, 9, 9))[at]
+        source = weight_first if at < 3 else weight_second
         return pltpu.make_async_copy(
-            source.at[pl.ds(low, count)],
-            taps_all.at[pl.ds(start, count), z, pl.ds(3 * core, 3)],
+            source.at[pl.ds(3 * (2 - at % 3), 3)],
+            taps_all.at[pl.ds(3 * at, 3), z, pl.ds(3 * core, 3)],
             load_sem.at[at],
         )
 
@@ -131,10 +131,9 @@
     lat_copy = pltpu.make_async_copy(
         latent, lat.at[pl.ds(2, frames), pl.ds(1, rows)], lat_sem
     )
-    load(0).start()
     lat_copy.start()
-    load(1).start()
-    load(2).start()
+    for at in range(UNITS // 3):
+        load(at).start()
     for copy in line_copies:
         copy.start()
 
@@ -144,10 +143,6 @@
         ({"group": group - 2}, z > 0),
         ({"group": group + 4}, z < zs - 2),
         ({"group": group - 4}, z > 1),
-        ({"tile": tile + 1, "group": group + 1}, (tile < tiles - 1) & (group < groups - 1)),
-        ({"tile": tile - 1, "group": group + 1}, (tile > 0) & (group < groups - 1)),
-        ({"tile": tile + 1, "group": group - 1}, (tile < tiles - 1) & (group > 0)),
-        ({"tile": tile - 1, "group": group - 1}, (tile > 0) & (group > 0)),
         ({"group": group + 1}, group < groups - 1),
         ({"group": group - 1}, group > 0),
         ({"tile": tile + 1}, tile < tiles - 1),
@@ -243,18 +238,16 @@
                 await_z(unit, z + steps * inward)
                 hand_on(unit, z + steps * inward)
 
-    def halo_copies(buf, which):
+    def halo_copies(buf, which, kind):
         late, low, high = pl.ds(frames, 2), tile > 0, tile < tiles - 1
-        sends, gets = group < groups - 1, group > 0
-        inner, body = pl.ds(1, rows), pl.ds(2, frames)
+        body = pl.ds(2, frames)
         plan = (
-            ((late, inner), (pl.ds(0, 2), inner), {"group": group + 1}, sends, gets),
             ((body, rows), (body, 0), {"tile": tile + 1}, high, low),
             ((body, 1), (body, rows + 1), {"tile": tile - 1}, low, high),
-            ((late, rows), (pl.ds(0, 2), 0), {"tile": tile + 1, "group": group + 1}, sends & high, gets & low),
-            ((late, 1), (pl.ds(0, 2), rows + 1), {"tile": tile - 1, "group": group + 1}, sends & low, gets & high),
+            ((late,), (pl.ds(0, 2),), {"group": group + 1}, group < groups - 1, group > 0),
         )
-        for at, (source, target, where, there, here) in enumerate(plan):
+        for at in (0, 1) if kind == "rows" else (2,):
+            source, target, where, there, here = plan[at]
             copy = pltpu.make_async_remote_copy(
                 src_ref=buf.at[source], dst_ref=buf.at[target],
                 send_sem=halo_send.at[which, at], recv_sem=halo_recv.at[which, at],
@@ -262,12 +255,12 @@
             )
             yield copy, there, here
 
-    def send_halo(buf, which):
-        for copy, there, _ in halo_copies(buf, which):
+    def send_halo(buf, which, kind):
+        for copy, there, _ in halo_copies(buf, which, kind):
             pl.when(there)(copy.start)
 
-    def await_halo(buf, which):
-        for copy, _, here in halo_copies(buf, which):
+    def await_halo(buf, which, kind):
+        for copy, _, here in halo_copies(buf, which, kind):
             pl.when(here)(copy.wait_recv)
 
     column = lax.broadcasted_iota(jnp.int32, (across, chans), 0)
@@ -300,21 +293,20 @@
         lax.fori_loop(low, high, step, 0)
 
     def multiply(unit):
-        step_t, step_r = (unit % 9) // 3, unit % 3
+        step_t, step_r = 2 - (unit % 9) // 3, unit % 3
         window = cols[pl.ds(step_t, frames), pl.ds(step_r, rows)].reshape(-1, 3 * chans)
         weight = taps_all[unit].reshape(3 * chans, chans)
         added = jnp.dot(window, weight, preferred_element_type=F32)
         total[...] += added.reshape(frames, rows, across, chans)
 
+    lat_copy.wait()
+    send_halo(lat, 0, "rows")
     load(0).wait()
-    own(0)
-    lat_copy.wait()
-    load(1).wait()
-    for unit in range(1, AHEAD):
+    for unit in range(AHEAD):
         own(unit)
-    send_halo(lat, 0)
     total[...] = jnp.zeros_like(total)
-    load(2).wait()
+    for at in range(1, UNITS // 3):
+        load(at).wait()
     for copy in line_copies:
         copy.wait()
 
@@ -391,16 +383,26 @@
 
         @pl.when(index == 1)
         def _():
-            await_halo(lat, 0)
-
-        @pl.when((index >= 1) & (index < frames + 3))
-        def _():
-            first_columns(index - 1)
+            await_halo(lat, 0, "rows")
+            send_halo(lat, 0, "frames")
+
+        @pl.when((index >= 1) & (index <= frames))
+        def _():
+            first_columns(index + 1)
+
+        @pl.when(index == frames + 1)
+        def _():
+            await_halo(lat, 0, "frames")
+            first_columns(0)
+
+        @pl.when(index == frames + 2)
+        def _():
+            first_columns(1)
 
         @pl.when(index == middle)
         def _():
             second_values()
-            send_halo(sec, 1)
+            send_halo(sec, 1, "rows")
 
         @pl.when(index == middle + 1)
         def _():
@@ -408,9 +410,14 @@
 
         @pl.when(index == middle + 2)
         def _():
-            await_halo(sec, 1)
+            await_halo(sec, 1, "rows")
+            send_halo(sec, 1, "frames")
+            second_columns(2, frames + 2, (0, rows + 1))
+
+        @pl.when(index == middle + 3)
+        def _():
+            await_halo(sec, 1, "frames")
             second_columns(0, 2, range(rows + 2))
-            second_columns(2, frames + 2, (0, rows + 1))
         return carry
 
     lax.fori_loop(0, turns, turn, 0)
@@ -427,8 +434,9 @@
         return carry
     lax.fori_loop(turns - drain_lag, UNITS, drain_rest, 0)
     for which, buf in enumerate((lat, sec)):
-        for copy, there, _ in halo_copies(buf, which):
-            pl.when(there)(copy.wait_send)
+        for kind in ("rows", "frames"):
+            for copy, there, _ in halo_copies(buf, which, kind):
+                pl.when(there)(copy.wait_send)
 
 
 def fused_local(latent, gain_first, weight_first, bias_first, gain_second, weight_second, bias_second):
@@ -448,7 +456,7 @@
             pltpu.VMEM((frames + 2, rows + 2, across, 3 * chans), BF16),
             pltpu.VMEM((frames, rows, across, chans), F32),
             *[pltpu.VMEM((chans,), F32)] * 4,
-            pltpu.SemaphoreType.DMA((3,)),
+            pltpu.SemaphoreType.DMA((UNITS // 3,)),
             pltpu.SemaphoreType.DMA,
             pltpu.SemaphoreType.DMA((4,)),
             pltpu.SemaphoreType.DMA((UNITS,)),
@@ -457,8 +465,8 @@
             pltpu.SemaphoreType.DMA((UNITS, 2)),
             pltpu.SemaphoreType.DMA((UNITS,)),
             pltpu.SemaphoreType.DMA((UNITS,)),
-            pltpu.SemaphoreType.DMA((2, 5)),
-            pltpu.SemaphoreType.DMA((2, 5)),
+            pltpu.SemaphoreType.DMA((2, 3)),
+            pltpu.SemaphoreType.DMA((2, 3)),
         ],
         compiler_params=pltpu.CompilerParams(
             collective_id=0, has_side_effects=True, vmem_limit_bytes=60 * 1024 * 1024

time: 80.2 us -> 75.9 us (0.946); the launches traced: 79.1 us -> 75.8 us
  Pallas kernels: 77.3 us -> 73.9 us
    pallas_call x1, Pallas kernels: 77.3 us -> 73.9 us  [fused_local(): pl.pallas_call(fused, out_shape=jax.ShapeDtypeStruct(latent.shape, BF16),...]
where the time goes in v7:
time: 75.9 us; the launch traced here: 75.8 us
  Pallas kernels  73.9 us (97%)
  local copies, waits for them, and re-layouts  1.82 us (2%)
    pallas_call x1, Pallas kernels, fused_local(): pl.pallas_call(fused, out_shape=jax.ShapeDtypeStruct(latent.shape, BF16),...  73.9 us
    unnamed x1, local copies, waits for them, and re-layouts  1.82 us

profile of v7, /device:TPU:27, one launch (start us, length us, event | category | flops | bytes accessed | tf_op | source)
XLA Modules:
  0.0 75.8 jit_solution(14318297851935920338)
XLA Ops:
  0.0 73.9 %shard_map.73 = bf16[4,3,48,384]{3,2,1,0:T(8,128)(2,1)} custom-call(bf16[4,3,48,384]{3,2,1,0:T(8,128)(2,1)} %latent.1, f32[384]{0:T(512)} %gain_first_in.1, bf16[9,3,48,384]{3,2,1,0:T(8,128)(2,1)} %bitcast.2, f32[384]{0:T(512)} %bias_first_in.1, f32[384]{0:T(512)} %gain_second_in.1, bf16[9,3,48,384]{3,2,1,0:T(8,128)(2,1)} %bitcast.3, f32[384]{0:T(512)} %bias_second_in.1), custom_call_target="tpu_custom_call" | custom-call | flops 9172942848 | bytes 2875392 | tf_op jit(solution)/shard_map/pallas_call | solution.py:447
  74.0 1.8 %copy.9 = bf16[4,3,48,384]{3,2,1,0:T(8,128)(2,1)} copy(bf16[4,3,48,384]{3,2,1,0:T(8,128)(2,1)} %shard_map.73) | data formatting | bytes 884736

commit v8 on v7

--- a/solution.py
+++ b/solution.py
@@ -365,19 +365,29 @@
     assert frames + 2 < first_lag
     middle = half - 1 + first_lag
     drain_lag = first_lag + 4
-    turns = UNITS + first_lag
+    turns = UNITS + first_lag - LAG
+
+    def reached(index, lag):
+        hurry = 2 * index - UNITS - 3 * (lag // LAG - 1)
+        return jnp.clip(jnp.maximum(index - lag + 1, hurry), 0, UNITS)
+
+    def steps(index, lag, body):
+        def step(unit, carry):
+            body(unit)
+            return carry
+        lax.fori_loop(reached(index - 1, lag), reached(index, lag), step, 0)
 
     def done_by(index):
         first = jnp.clip(index - first_lag + 1, 0, half)
-        second = jnp.clip(jnp.minimum(2 * (index - middle - 2), index - first_lag - half + 1), 0, half)
+        second = jnp.clip(jnp.minimum(2 * (index - middle - 2), reached(index - 1, forward_lag) - half), 0, half)
         return first + second
 
     def turn(index, carry):
         stage(index, -AHEAD, own)
         stage(index, 0, near)
-        stage(index, LAG, far)
-        stage(index, direct_lag, direct)
-        stage(index, forward_lag, forwarded)
+        steps(index, LAG, far)
+        steps(index, direct_lag, direct)
+        steps(index, forward_lag, forwarded)
         stage(index, drain_lag, drain)
         lax.fori_loop(done_by(index - 1), done_by(index), compute, 0)
 
@@ -469,7 +479,7 @@
             pltpu.SemaphoreType.DMA((2, 3)),
         ],
         compiler_params=pltpu.CompilerParams(
-            collective_id=0, has_side_effects=True, vmem_limit_bytes=60 * 1024 * 1024
+            collective_id=0, has_side_effects=True, vmem_limit_bytes=56 * 1024 * 1024
         ),
         cost_estimate=pl.CostEstimate(
             flops=4 * frames * rows * across * 27 * chans * chans,

time: 75.9 us -> 77.1 us (1.016)
  Pallas kernels: 73.9 us -> 75.1 us
    pallas_call x1, Pallas kernels: 73.9 us -> 75.1 us  [fused_local(): pl.pallas_call(fused, out_shape=jax.ShapeDtypeStruct(latent.shape, BF16),...]
where the time goes in v8:
time: 77.1 us; the launch traced here: 76.9 us
  Pallas kernels  75.1 us (97%)
  local copies, waits for them, and re-layouts  1.82 us (2%)
    pallas_call x1, Pallas kernels, fused_local(): pl.pallas_call(fused, out_shape=jax.ShapeDtypeStruct(latent.shape, BF16),...  75.1 us
    unnamed x1, local copies, waits for them, and re-layouts  1.82 us

profile of v8, /device:TPU:27, one launch (start us, length us, event | category | flops | bytes accessed | tf_op | source)
XLA Modules:
  0.0 76.9 jit_solution(17620218069448470674)
XLA Ops:
  0.0 75.1 %shard_map.73 = bf16[4,3,48,384]{3,2,1,0:T(8,128)(2,1)} custom-call(bf16[4,3,48,384]{3,2,1,0:T(8,128)(2,1)} %latent.1, f32[384]{0:T(512)} %gain_first_in.1, bf16[9,3,48,384]{3,2,1,0:T(8,128)(2,1)} %bitcast.2, f32[384]{0:T(512)} %bias_first_in.1, f32[384]{0:T(512)} %gain_second_in.1, bf16[9,3,48,384]{3,2,1,0:T(8,128)(2,1)} %bitcast.3, f32[384]{0:T(512)} %bias_second_in.1), custom_call_target="tpu_custom_call" | custom-call | flops 9172942848 | bytes 2875392 | tf_op jit(solution)/shard_map/pallas_call | solution.py:457
  75.1 1.8 %copy.9 = bf16[4,3,48,384]{3,2,1,0:T(8,128)(2,1)} copy(bf16[4,3,48,384]{3,2,1,0:T(8,128)(2,1)} %shard_map.73) | data formatting | bytes 884736

commit v9 on v7

--- a/solution.py
+++ b/solution.py
@@ -359,10 +359,10 @@
         across_cores(unit).wait_send()
 
     half = UNITS // 2
-    direct_lag = 2 * LAG
+    direct_lag = 2 * LAG - 1
     forward_lag = direct_lag + LAG
     first_lag = forward_lag + 1
-    assert frames + 2 < first_lag
+    assert frames < first_lag
     middle = half - 1 + first_lag
     drain_lag = first_lag + 4
     turns = UNITS + first_lag
@@ -376,10 +376,10 @@
         stage(index, -AHEAD, own)
         stage(index, 0, near)
         stage(index, LAG, far)
-        stage(index, direct_lag, direct)
         stage(index, forward_lag, forwarded)
         stage(index, drain_lag, drain)
         lax.fori_loop(done_by(index - 1), done_by(index), compute, 0)
+        stage(index, direct_lag, direct)
 
         @pl.when(index == 1)
         def _():

time: 75.9 us -> 78 us (1.028)
  Pallas kernels: 73.9 us -> 76 us
    pallas_call x1, Pallas kernels: 73.9 us -> 76 us  [fused_local(): pl.pallas_call(fused, out_shape=jax.ShapeDtypeStruct(latent.shape, BF16),...]
where the time goes in v9:
time: 78 us; the launch traced here: 77.9 us
  Pallas kernels  76 us (97%)
  local copies, waits for them, and re-layouts  1.82 us (2%)
    pallas_call x1, Pallas kernels, fused_local(): pl.pallas_call(fused, out_shape=jax.ShapeDtypeStruct(latent.shape, BF16),...  76 us
    unnamed x1, local copies, waits for them, and re-layouts  1.82 us

profile of v9, /device:TPU:27, one launch (start us, length us, event | category | flops | bytes accessed | tf_op | source)
XLA Modules:
  0.0 77.9 jit_solution(15269391004016234032)
XLA Ops:
  0.0 76.0 %shard_map.73 = bf16[4,3,48,384]{3,2,1,0:T(8,128)(2,1)} custom-call(bf16[4,3,48,384]{3,2,1,0:T(8,128)(2,1)} %latent.1, f32[384]{0:T(512)} %gain_first_in.1, bf16[9,3,48,384]{3,2,1,0:T(8,128)(2,1)} %bitcast.2, f32[384]{0:T(512)} %bias_first_in.1, f32[384]{0:T(512)} %gain_second_in.1, bf16[9,3,48,384]{3,2,1,0:T(8,128)(2,1)} %bitcast.3, f32[384]{0:T(512)} %bias_second_in.1), custom_call_target="tpu_custom_call" | custom-call | flops 9172942848 | bytes 2875392 | tf_op jit(solution)/shard_map/pallas_call | solution.py:447
  76.0 1.8 %copy.9 = bf16[4,3,48,384]{3,2,1,0:T(8,128)(2,1)} copy(bf16[4,3,48,384]{3,2,1,0:T(8,128)(2,1)} %shard_map.73) | data formatting | bytes 884736

commit v10 on v7

--- a/solution.py
+++ b/solution.py
@@ -77,7 +77,7 @@
 BF16, F32 = jnp.bfloat16, jnp.float32
 MESH = pl.DeviceIdType.MESH
 UNITS = 18
-AHEAD = 3
+AHEAD = 2
 LAG = 2
 
 

time: 75.9 us -> 75.9 us (level)
  no operation moved by 1% of the time
where the time goes in v10:
time: 75.9 us; the launch traced here: 75.7 us
  Pallas kernels  73.9 us (97%)
  local copies, waits for them, and re-layouts  1.82 us (2%)
    pallas_call x1, Pallas kernels, fused_local(): pl.pallas_call(fused, out_shape=jax.ShapeDtypeStruct(latent.shape, BF16),...  73.9 us
    unnamed x1, local copies, waits for them, and re-layouts  1.82 us

profile of v10, /device:TPU:27, one launch (start us, length us, event | category | flops | bytes accessed | tf_op | source)
XLA Modules:
  0.0 75.7 jit_solution(11688078547120835979)
XLA Ops:
  0.0 73.9 %shard_map.73 = bf16[4,3,48,384]{3,2,1,0:T(8,128)(2,1)} custom-call(bf16[4,3,48,384]{3,2,1,0:T(8,128)(2,1)} %latent.1, f32[384]{0:T(512)} %gain_first_in.1, bf16[9,3,48,384]{3,2,1,0:T(8,128)(2,1)} %bitcast.2, f32[384]{0:T(512)} %bias_first_in.1, f32[384]{0:T(512)} %gain_second_in.1, bf16[9,3,48,384]{3,2,1,0:T(8,128)(2,1)} %bitcast.3, f32[384]{0:T(512)} %bias_second_in.1), custom_call_target="tpu_custom_call" | custom-call | flops 9172942848 | bytes 2875392 | tf_op jit(solution)/shard_map/pallas_call | solution.py:447
  73.9 1.8 %copy.9 = bf16[4,3,48,384]{3,2,1,0:T(8,128)(2,1)} copy(bf16[4,3,48,384]{3,2,1,0:T(8,128)(2,1)} %shard_map.73) | data formatting | bytes 884736
